TPU v7x, 256 devices: a whole 4x4x8 slice. The times are simulated.
256 devices in a mesh: hid: 16 (over y, x_lo, core), wid: 16 (over z, x_hi).
Axes of the slice: x: 4 (x_hi: 2, x_lo: 2; x = x_hi * 2 + x_lo), y: 4, z: 8, core: 2. Of those that a mesh axis runs over, the one named last changes fastest.
Arguments:
- tokens: bfloat16 [512, 8192], P('hid', 'wid'), may hold values from -6 to 6
- out_grad: bfloat16 [512, 8192], P('hid', 'wid'), may hold values from -6 to 6
- gate_weight: bfloat16 [8192, 28672], P('wid', 'hid'), may hold values from -0.0625 to 0.0625
- up_weight: bfloat16 [8192, 28672], P('wid', 'hid'), may hold values from -0.0625 to 0.0625
- down_weight: bfloat16 [28672, 8192], P('hid', 'wid'), may hold values from -0.03125 to 0.03125
- cap_codes: int32 [28672], P('hid'), may hold values from 256 to 2048
Outputs:
- input_grad: bfloat16 [512, 8192], P('hid', 'wid')
- gate_grad: bfloat16 [8192, 28672], P('wid', 'hid')
- up_grad: bfloat16 [8192, 28672], P('wid', 'hid')
- down_grad: bfloat16 [28672, 8192], P('hid', 'wid')
Inputs may be any that keep to these rules, and one draw needn't show every extreme that they name: `cap_codes`: each hidden unit's cap is its code divided by 512.
All inputs are finite; a program needn't handle non-finite values.
Results may differ from a plain program's by a relative error of at most 0.005.
Values may be sent and summed in bfloat16 or wider, within the bound.
A program may use at most 128 MiB of HBM per device.

v0:
```python
import jax
import jax.numpy as jnp
from jax import lax
from jax.sharding import PartitionSpec as P


def contract_last(left, right):
    return lax.dot_general(
        left, right, (((1,), (1,)), ((), ())), preferred_element_type=jnp.float32
    )


def contract_first(left, right):
    return lax.dot_general(
        left, right, (((0,), (0,)), ((), ())), preferred_element_type=jnp.float32
    )


def local_step(gate, up, cap_grad, cap_vals):
    sigmoid_gate = jax.nn.sigmoid(gate)
    active = gate * sigmoid_gate
    squash = jnp.tanh(active * up / cap_vals[None, :])
    capped = (cap_vals[None, :] * squash).astype(jnp.bfloat16)
    hidden_grad = cap_grad * (1.0 - squash * squash)
    gate_delta = (hidden_grad * up * sigmoid_gate * (1.0 + gate * (1.0 - sigmoid_gate))).astype(
        jnp.bfloat16
    )
    up_delta = (hidden_grad * active).astype(jnp.bfloat16)
    return (capped, gate_delta, up_delta)


def per_device(tokens, out_grad, gate_weight, up_weight, down_weight, cap_codes):
    tok_panel, grad_panel = (
        lax.all_gather(tokens, "hid", axis=0, tiled=True),
        lax.all_gather(out_grad, "hid", axis=0, tiled=True),
    )
    hid_cols = gate_weight.shape[1]
    cap_all = cap_codes.astype(jnp.float32) * (1.0 / 512.0)
    rows_in = tok_panel
    front = lax.psum_scatter(
        jnp.concatenate(
            [
                jnp.dot(rows_in, gate_weight, preferred_element_type=jnp.float32),
                jnp.dot(rows_in, up_weight, preferred_element_type=jnp.float32),
            ],
            axis=1,
        ),
        "wid",
        scatter_dimension=0,
        tiled=True,
    )
    rows_in = grad_panel
    cap_grad = lax.psum_scatter(
        contract_last(rows_in, down_weight), "wid", scatter_dimension=0, tiled=True
    )
    gate = front[:, :hid_cols]
    up = front[:, hid_cols:]
    capped, gate_delta, up_delta = local_step(gate, up, cap_grad, cap_all)
    capped_full, gate_full, up_full = (
        lax.all_gather(capped, "wid", axis=0, tiled=True),
        lax.all_gather(gate_delta, "wid", axis=0, tiled=True),
        lax.all_gather(up_delta, "wid", axis=0, tiled=True),
    )
    input_grad = lax.psum_scatter(
        contract_last(gate_full, gate_weight) + contract_last(up_full, up_weight),
        "hid",
        scatter_dimension=0,
        tiled=True,
    ).astype(jnp.bfloat16)
    gate_grad = contract_first(tok_panel, gate_full).astype(jnp.bfloat16)
    up_grad = contract_first(tok_panel, up_full).astype(jnp.bfloat16)
    down_grad = contract_first(capped_full, grad_panel).astype(jnp.bfloat16)
    return (input_grad, gate_grad, up_grad, down_grad)


def solution(mesh):
    return jax.shard_map(
        per_device,
        mesh=mesh,
        in_specs=(
            P("hid", "wid"),
            P("hid", "wid"),
            P("wid", "hid"),
            P("wid", "hid"),
            P("hid", "wid"),
            P("hid"),
        ),
        out_specs=(P("hid", "wid"), P("wid", "hid"), P("wid", "hid"), P("hid", "wid")),
        check_vma=False,
    )
```

profile of v0, /device:TPU:17, one launch (start us, length us, event | category | flops | bytes accessed | tf_op | source)
XLA Modules:
  0.0 788.6 jit_solution(17260568071357159556)
XLA Ops:
  7.2 0.0 copy-start
  7.2 0.0 reduce-scatter.6.cloned.1.call-start
  7.2 18.7 %all_gather.16 = bf16[512,512]{1,0:T(8,128)(2,1)S(1)} all-gather(bf16[32,512]{1,0:T(8,128)(2,1)} %param.6), channel_id=1, replica_groups=mesh['hid'=16,'wid'=16] {'hid'}, dimensions={0}, use_global_device_ids=true | all-gather | bytes 557056 | tf_op jit(solution)/shard_map/all_gather | solution.py:34
  25.9 0.0 copy-done
  26.0 0.0 copy-start.1
  26.0 1.1 fusion.4
  27.1 0.4 copy-done.1
  27.5 1.1 fusion.5
  28.6 4.0 pad_maximum_fusion
  32.6 0.0 copy-start.2
  32.6 0.0 reduce-scatter.6.cloned.1.call-update
  32.6 0.0 reduce-scatter.4.cloned.1.call-start
  32.7 0.7 copy-done.2
  33.3 18.4 %all_gather.15 = bf16[512,512]{1,0:T(8,128)(2,1)S(1)} all-gather(bf16[32,512]{1,0:T(8,128)(2,1)S(1)} %copy-done.2), channel_id=1, replica_groups=mesh['hid'=16,'wid'=16] {'hid'}, dimensions={0}, use_global_device_ids=true | all-gather | bytes 557056 | tf_op jit(solution)/shard_map/all_gather | solution.py:35
  51.7 4.6 fusion.3
  56.3 0.0 copy-start.3
  56.3 0.0 reduce-scatter.4.cloned.1.call-update
  56.3 0.0 all-gather.4.cloned.1.call-start
  56.3 0.6 copy-done.3
  57.0 200.6 %reduce-scatter.6.cloned.1.call-done = f32[32,3584]{1,0:T(8,128)} async-done(((f32[512,3584]{1,0:T(8,128)}), f32[32,3584]{1,0:T(8,128)}) %reduce-scatter.6.cloned.1.call-update) | async-done | bytes 458768 | tf_op jit(solution)/shard_map/reduce_scatter | solution.py:40
  257.6 1.8 multiply_convert_fusion
  259.4 212.5 %reduce-scatter.4.cloned.1.call-done = f32[32,1792]{1,0:T(8,128)} async-done(((f32[512,1792]{1,0:T(8,128)}), f32[32,1792]{1,0:T(8,128)}) %reduce-scatter.4.cloned.1.call-update) | async-done | bytes 229392 | tf_op jit(solution)/shard_map/reduce_scatter | solution.py:53
  471.9 2.0 multiply_convert_fusion.1
  473.9 0.0 all-gather.4.cloned.1.call-update
  473.9 0.0 all-gather.6.cloned.1.call-start
  474.0 0.5 all-gather.6.cloned.1.call-update
  474.5 0.0 all-gather.8.cloned.1.call-start
  474.5 0.5 all-gather.8.cloned.1.call-update
  475.1 0.0 reduce-scatter.8.cloned.1.call-start
  475.1 82.5 %all-gather.4.cloned.1.call-done = bf16[512,1792]{1,0:T(8,128)(2,1)} async-done(((bf16[32,1792]{1,0:T(8,128)(2,1)}), bf16[512,1792]{1,0:T(8,128)(2,1)}) %all-gather.4.cloned.1.call-update) | async-done | bytes 1835024 | tf_op jit(solution)/shard_map/all_gather | solution.py:61
  557.6 3.6 fusion.6
  561.2 80.1 %all-gather.6.cloned.1.call-done = bf16[512,1792]{1,0:T(8,128)(2,1)} async-done(((bf16[32,1792]{1,0:T(8,128)(2,1)}), bf16[512,1792]{1,0:T(8,128)(2,1)}) %all-gather.6.cloned.1.call-update) | async-done | bytes 1835024 | tf_op jit(solution)/shard_map/all_gather | solution.py:62
  641.3 4.5 convolution_add_fusion
  645.8 0.0 reduce-scatter.8.cloned.1.call-update
  645.8 3.9 fusion
  649.7 3.8 copy.10
  653.5 3.9 fusion.1
  657.4 3.8 copy.11
  661.2 63.3 %all-gather.8.cloned.1.call-done = bf16[512,1792]{1,0:T(8,128)(2,1)} async-done(((bf16[32,1792]{1,0:T(8,128)(2,1)}), bf16[512,1792]{1,0:T(8,128)(2,1)}) %all-gather.8.cloned.1.call-update) | async-done | bytes 1835024 | tf_op jit(solution)/shard_map/all_gather | solution.py:60
  724.5 3.9 convolution_convert_fusion
  728.4 51.9 %reduce-scatter.8.cloned.1.call-done = f32[32,512]{1,0:T(8,128)} async-done(((f32[512,512]{1,0:T(8,128)}), f32[32,512]{1,0:T(8,128)}) %reduce-scatter.8.cloned.1.call-update) | async-done | bytes 65552 | tf_op jit(solution)/shard_map/reduce_scatter | solution.py:64
  780.3 1.5 convert_element_type.33
  (1 shorter events, 0.0 us)
Async XLA Ops:
  7.2 18.8 %copy-start = (bf16[512,1792]{1,0:T(8,128)(2,1)S(1)}, bf16[512,1792]{1,0:T(8,128)(2,1)}, u32[]{:S(2)}) copy-start(bf16[512,1792]{1,0:T(8,128)(2,1)} %param.8) | copy-start | bytes 5505028
  7.2 250.4 %reduce-scatter.6.cloned.1.call-start = ((), (), s32[]{:S(2)}) async-start(), calls=%async_computation.4 | async-start | bytes 7798784 | tf_op jit(solution)/shard_map/reduce_scatter | solution.py:40
  26.0 1.5 copy-start.1
  32.6 0.8 copy-start.2
  32.6 439.3 %reduce-scatter.4.cloned.1.call-start = ((), (), s32[]{:S(2)}) async-start(), calls=%async_computation.3 | async-start | bytes 3899392 | tf_op jit(solution)/shard_map/reduce_scatter | solution.py:53
  56.3 0.7 copy-start.3
  56.3 501.3 %all-gather.4.cloned.1.call-start = ((), (), s32[]{:S(2)}) async-start(), calls=%async_computation.5 | async-start | bytes 1949696 | tf_op jit(solution)/shard_map/all_gather | solution.py:61
  473.9 167.4 %all-gather.6.cloned.1.call-start = ((), (), s32[]{:S(2)}) async-start(), calls=%async_computation.6 | async-start | bytes 1949696 | tf_op jit(solution)/shard_map/all_gather | solution.py:62
  474.5 250.0 %all-gather.8.cloned.1.call-start = ((), (), s32[]{:S(2)}) async-start(), calls=%async_computation.8 | async-start | bytes 1949696 | tf_op jit(solution)/shard_map/all_gather | solution.py:60
  475.1 305.2 %reduce-scatter.8.cloned.1.call-start = ((), (), s32[]{:S(2)}) async-start(), calls=%async_computation.7 | async-start | bytes 1114112 | tf_op jit(solution)/shard_map/reduce_scatter | solution.py:64
Sparse Core Ops, SparseCore 0:
  32.7 224.7 reduce-scatter.5
  262.1 209.7 reduce-scatter.3
  475.1 82.4 all-gather.3
  560.6 80.6 all-gather.5
  643.8 80.6 all-gather.7
  726.8 53.3 reduce-scatter.7
where the time goes:
time: 800 us; the launch traced here: 789 us
  waiting for transfers between devices  692 us (86%)
  blocking collectives  37.1 us (5%)
  matrix products  26.5 us (3%)
  between operations  14.1 us (2%)
  local copies, waits for them, and re-layouts  9.31 us (1%)
  other arithmetic  9.25 us (1%)
    reduce_scatter x1, waiting for transfers between devices, per_device(): lax.psum_scatter(contract_last(rows_in, down_weight), 'wid', scatter_dime...  213 us
    reduce_scatter x1, waiting for transfers between devices, per_device(): lax.psum_scatter(jnp.concatenate([jnp.dot(rows_in, gate_weight, preferred...  201 us
    all_gather x1, waiting for transfers between devices, per_device(): lax.all_gather(gate_delta, 'wid', axis=0, tiled=True)  82.5 us
    all_gather x1, waiting for transfers between devices, per_device(): lax.all_gather(up_delta, 'wid', axis=0, tiled=True)  80.1 us
    all_gather x1, waiting for transfers between devices, per_device(): lax.all_gather(capped, 'wid', axis=0, tiled=True)  63.3 us
    reduce_scatter x1, waiting for transfers between devices, per_device(): lax.psum_scatter(contract_last(gate_full, gate_weight) + contract_last(up...  51.9 us
    all_gather x1, blocking collectives, per_device(): lax.all_gather(tokens, 'hid', axis=0, tiled=True)  18.7 us
    all_gather x1, blocking collectives, per_device(): lax.all_gather(out_grad, 'hid', axis=0, tiled=True)  18.4 us
  transfers between devices with their start and end apart: 6, of which 6 were waited for; matrix products, arithmetic and copies ran while one was open for 4% of the time, Pallas kernels for 0%

commit v1 on v0

v1 whole, which is shorter than its diff:
```python
import functools

import jax
import jax.numpy as jnp
from jax import lax
from jax.experimental import pallas as pl
from jax.experimental.pallas import tpu as pltpu
from jax.sharding import PartitionSpec as P

MESH = pl.DeviceIdType.MESH
BF16 = jnp.bfloat16
F32 = jnp.float32

TILE = 256
NB = 32
NZ = 8
SCALE = 2.0**18


def dot(a, b, ca, cb):
    return lax.dot_general(a, b, (((ca,), (cb,)), ((), ())), preferred_element_type=F32)


def enc(v):
    u = v * SCALE
    return ((u * jnp.abs(u)) * (u * u)).astype(BF16)


def dec(y):
    y = y.astype(F32)
    root = lax.rsqrt(lax.rsqrt(jnp.maximum(jnp.abs(y), 2e-38)))
    return root * jnp.where(y < 0.0, -1.0 / SCALE, 1.0 / SCALE)


def kernel(
    na, nb,
    tok_in, og_in, gw_in, uw_in, dw_in, cap_in,
    d_out, panel_out, ig_out,
    gw, uw, dw, panel,
    pa, pb, xa_s, xa_r, sa, ra, sb, rb, xb_s, xb_r,
    ga, gb, ig_acc, sib_s, sib_r, ig_s, ig_r,
    lsem, dsem, tok_ss, tok_rs, fwd_ss, fwd_rs, xa_ss, xa_rs, za_ss, za_rs, zb_ss, zb_rs, xb_ss, xb_rs,
    gxa_ss, gxa_rs, gza_ss, gza_rs, gzb_ss, gzb_rs, gxb_ss, gxb_rs, sib_ss, sib_rs, ig_ss, ig_rs,
):
    wa, wb = na * TILE, nb * TILE
    h, w = lax.axis_index("hid"), lax.axis_index("wid")
    z, xh = w // 2, w % 2
    xo = 1 - xh
    q, core = h // 2, h % 2
    zp = lambda k: (z + k + NZ) % NZ
    up_dev, dn_dev, x_dev = (h, zp(1) * 2 + xh), (h, zp(-1) * 2 + xh), (h, z * 2 + xo)
    z_dev = (dn_dev, up_dev)
    sib_dev = (q * 2 + 1 - core, w)
    chip = lambda j: (q + j + 8) % 8
    peer = lambda j: (chip(j) * 2 + core, w)

    def remote(src, dst, ss, rs, dev):
        return pltpu.make_async_remote_copy(
            src_ref=src, dst_ref=dst, send_sem=ss, recv_sem=rs, device_id=dev, device_id_type=MESH
        )

    loads = [
        pltpu.make_async_copy(tok_in, panel.at[0, q, core], lsem.at[0]),
        pltpu.make_async_copy(og_in, panel.at[1, q, core], lsem.at[1]),
        pltpu.make_async_copy(gw_in, gw, lsem.at[2]),
        pltpu.make_async_copy(uw_in, uw, lsem.at[3]),
        pltpu.make_async_copy(dw_in, dw, lsem.at[4]),
    ]
    for c in loads:
        c.start()

    bar = pltpu.get_barrier_semaphore()
    for dev in (up_dev, dn_dev, x_dev, sib_dev):
        pl.semaphore_signal(bar, inc=1, device_id=dev, device_id_type=MESH)
    for j in range(1, 8):
        pl.semaphore_signal(bar, inc=1, device_id=peer(j), device_id_type=MESH)
    pl.semaphore_wait(bar, 11)

    def tok_copy(p, j):
        mine = panel.at[p, q, core]
        return remote(mine, mine, tok_ss.at[p, j], tok_rs.at[p, j], peer(j))

    def fwd_copy(p, j):
        blk = panel.at[p, chip(-j), core]
        return remote(blk, blk, fwd_ss.at[p, j], fwd_rs.at[p, j], sib_dev)

    def fwd_got(p, j):
        blk = panel.at[p, chip(-j), 1 - core]
        return remote(blk, blk, fwd_ss.at[p, j], fwd_rs.at[p, j], sib_dev)

    for p in range(2):
        loads[p].wait()

        @pl.loop(1, 8)
        def _(j, p=p):
            tok_copy(p, j).start()

        fwd_copy(p, 0).start()

    def gather(p):
        @pl.loop(1, 8)
        def _(j):
            tok_copy(p, j).wait_recv()
            fwd_copy(p, j).start()

        @pl.loop(0, 8)
        def _(j):
            fwd_got(p, j).wait_recv()

    def partial(m, rows, col):
        if m == 2:
            return dot(rows, dw[pl.ds(col, TILE), :], 1, 1)
        return dot(rows, (gw, uw)[m][:, pl.ds(col, TILE)], 1, 0)

    def tile(i):
        return pl.ds(pl.multiple_of(i * TILE, TILE), TILE)

    def part_a(ms, dst, x, f):
        @pl.loop(0, na)
        def _(i):
            for m in ms:
                rows = panel[m // 2, :, x].reshape(NZ * NB, 512)
                dst[:, m, :, tile(i)] = f(partial(m, rows, pl.multiple_of(i * TILE, TILE))).reshape(NZ, NB, TILE)

    def part_b(ms):
        @pl.loop(0, nb)
        def _(i):
            for m in ms:
                rows = panel[m // 2].reshape(2 * NZ * NB, 512)
                v = partial(m, rows, pl.multiple_of(wa + i * TILE, TILE)).reshape(NZ, 2, NB, TILE)
                for x in range(2):
                    pb[:, 3 * x + m, :, tile(i)] = v[:, x]

    def xa_copy(k, g):
        d = zp(k)
        ms = (pl.ds(0, 2), pl.ds(2, 1))[g]
        return remote(xa_s.at[d, ms], xa_r.at[d, ms], xa_ss.at[g, d], xa_rs.at[g, d], x_dev)

    order = (4, 3, -3, 2, -2, 1, -1, 0)
    gather(0)
    loads[2].wait()
    loads[3].wait()
    part_a((0, 1), xa_s, xo, enc)
    for k in order[:2]:
        xa_copy(k, 0).start()
    part_b((0, 1))
    part_a((0, 1), pa, xh, lambda v: v)
    gather(1)
    loads[4].wait()
    part_a((2,), xa_s, xo, enc)
    for k in order[:2]:
        xa_copy(k, 1).start()
    for k in order[2:]:
        for g in range(2):
            xa_copy(k, g).start()
    part_b((2,))

    def hop(dst, own, recv, lo, hi):
        width = own.shape[-1] // 2

        @pl.loop(0, own.shape[0])
        def _(m):
            @pl.loop(lo, hi)
            def _(i):
                c = pl.ds(pl.multiple_of(i * width, 128), width)
                v = own[m, :, c]
                for r in recv:
                    v = v + dec(r[m, :, c])
                dst[m, :, c] = enc(v) if dst.dtype == BF16 else v

    class Ring:
        def __init__(self, own, s, r, ss, rs):
            self.own, self.s, self.r, self.ss, self.rs = own, s, r, ss, rs
            self.half = own.shape[-1] // 2

        def copy(self, step, d):
            src, dst = self.s.at[d, step - 1], self.r.at[d, step - 1]
            if step == 1:
                c = pl.ds(d * self.half, self.half)
                src, dst = src.at[:, :, c], dst.at[:, :, c]
            return remote(src, dst, self.ss.at[d, step - 1], self.rs.at[d, step - 1], z_dev[d])

        def step(self, step):
            for d in range(2):
                own = self.own.at[zp((5 - step) * (-1, 1)[d])]
                src = self.s.at[d, step - 1]
                if step == 1:
                    hop(src, own, (), d, d + 1)
                else:
                    self.copy(step - 1, d).wait_recv()
                    got = self.r.at[d, step - 2]
                    if step == 2:
                        hop(src, own, (got,), d, d + 1)
                        hop(src, own, (), 1 - d, 2 - d)
                    else:
                        hop(src, own, (got,), 0, 2)
                self.copy(step, d).start()

        def finish(self, dst):
            for d in range(2):
                self.copy(4, d).wait_recv()
            hop(dst, self.own.at[z], (self.r.at[0, 3], self.r.at[1, 3]), 0, 2)

        def drain(self):
            for d in range(2):
                for step in range(1, 5):
                    self.copy(step, d).wait_send()

    ring_a = Ring(pa, sa, ra, za_ss, za_rs)
    ring_b = Ring(pb, sb, rb, zb_ss, zb_rs)

    ring_b.step(1)
    part_a((2,), pa, xh, lambda v: v)

    def take_x(k):
        for g in range(2):
            xa_copy(k, g).wait_recv()
        d = zp(k)
        hop(pa.at[d], pa.at[d], (xa_r.at[d],), 0, 2)

    take_x(4)
    ring_a.step(1)
    for s, ks in ((2, (3, -3)), (3, (2, -2)), (4, (1, -1))):
        ring_b.step(s)
        for k in ks:
            take_x(k)
        ring_a.step(s)
    ring_b.finish(pb.at[z])
    hop(xb_s, pb.at[z, pl.ds(3 * xo, 3)], (), 0, 2)
    xb_copy = remote(xb_s, xb_r, xb_ss, xb_rs, x_dev)
    xb_copy.start()
    take_x(0)
    ring_a.finish(pa.at[z])

    def local(src, dst, n, base):
        @pl.loop(0, n)
        def _(i):
            gate, up, cap_grad = src[0, :, tile(i)], src[1, :, tile(i)], src[2, :, tile(i)]
            at = 2 * (base + i)
            codes = jnp.concatenate([cap_in[pl.ds(at, 1), :], cap_in[pl.ds(at + 1, 1), :]], axis=1)
            cap = codes.astype(F32) * (1.0 / 512.0)
            sig = 1.0 / (1.0 + jnp.exp(-gate))
            act = gate * sig
            squash = jnp.tanh(act * up / cap)
            hid_grad = cap_grad * (1.0 - squash * squash)
            dst[0, :, tile(i)] = (cap * squash).astype(BF16)
            dst[1, :, tile(i)] = (hid_grad * up * sig * (1.0 + gate * (1.0 - sig))).astype(BF16)
            dst[2, :, tile(i)] = (hid_grad * act).astype(BF16)

    local(pa.at[z], ga.at[z, xh], na, 0)

    def halves(blk, step, d, width):
        return blk.at[:, :, pl.ds(d * (width // 2), width // 2)] if step == 4 else blk

    def gza_copy(step, d, got=False):
        blk = halves(ga.at[zp((step if got else step - 1) * (1, -1)[d]), xh], step, d, wa)
        return remote(blk, blk, gza_ss.at[d, step - 1], gza_rs.at[d, step - 1], z_dev[d])

    def gxa_copy(k, got=False):
        blk = ga.at[zp(k), xo if got else xh]
        return remote(blk, blk, gxa_ss.at[zp(k)], gxa_rs.at[zp(k)], x_dev)

    def gzb_copy(step, d, got=False):
        blk = halves(gb.at[zp((step if got else step - 1) * (1, -1)[d])], step, d, wb)
        return remote(blk, blk, gzb_ss.at[d, step - 1], gzb_rs.at[d, step - 1], z_dev[d])

    def keep_a(k, x):
        d = zp(k)
        t = pl.multiple_of((d * 2 + x) * NB, NB)
        return pltpu.make_async_copy(ga.at[d, x], d_out.at[:, pl.ds(t, NB), pl.ds(0, wa)], dsem.at[0, d, x])

    def keep_b(k, x):
        d = zp(k)
        t = pl.multiple_of((d * 2 + x) * NB, NB)
        return pltpu.make_async_copy(
            gb.at[d, pl.ds(3 * x, 3)], d_out.at[:, pl.ds(t, NB), pl.ds(wa, wb)], dsem.at[1, d, x]
        )

    def keep_bs(k):
        for x in range(2):
            keep_b(k, x).start()

    for d in range(2):
        gza_copy(1, d).start()
    gxa_copy(0).start()
    keep_a(0, xh).start()
    keep_panel = pltpu.make_async_copy(panel, panel_out, lsem.at[0])
    keep_panel.start()

    xb_copy.wait()
    own_b = pb.at[z, pl.ds(3 * xh, 3)]
    hop(own_b, own_b, (xb_r,), 0, 2)
    local(own_b, gb.at[z, pl.ds(3 * xh, 3)], nb, na)

    def gxb_copy(x):
        blk = gb.at[z, pl.ds(3 * x, 3)]
        return remote(blk, blk, gxb_ss, gxb_rs, x_dev)

    gxb_copy(xh).start()

    @pl.loop(0, NZ * 2)
    def _(i):
        ig_acc[i // 2, i % 2] = jnp.zeros((NB, 512), F32)

    def ig_rows(ks):
        def rows(ref, m, i):
            return jnp.concatenate([ref(zp(k), x, m, i) for k in ks for x in range(2)], axis=0)

        def run(ref, n, base):
            @pl.loop(0, n)
            def _(i):
                c = tile(base + i)
                v = dot(rows(ref, 1, i), gw[:, c], 1, 1) + dot(rows(ref, 2, i), uw[:, c], 1, 1)
                for n_k, k in enumerate(ks):
                    ig_acc[zp(k)] += v[n_k * 2 * NB : (n_k + 1) * 2 * NB].reshape(2, NB, 512)

        run(lambda d, x, m, i: ga[d, x, m, :, tile(i)], na, 0)
        run(lambda d, x, m, i: gb[d, 3 * x + m, :, tile(i)], nb, na)
        for k in ks:
            d = zp(k)
            sib_s[d] = ig_acc[d, 1 - core].astype(BF16)
            sib_copy(d).start()

    def sib_copy(d):
        return remote(sib_s.at[d], sib_r.at[d], sib_ss.at[d], sib_rs.at[d], sib_dev)

    def take_gx(k):
        gxa_copy(k, True).wait_recv()
        keep_a(k, xo).start()

    for step in range(2, 5):
        for d in range(2):
            k = (step - 1) * (1, -1)[d]
            gza_copy(step - 1, d, True).wait_recv()
            gza_copy(step, d).start()
            gxa_copy(k).start()
            keep_a(k, xh).start()
        if step == 2:
            gxb_copy(xo).wait_recv()
            keep_bs(0)
        for d in range(2):
            if step > 2:
                gzb_copy(step - 2, d, True).wait_recv()
                keep_bs((step - 2) * (1, -1)[d])
            gzb_copy(step - 1, d).start()
    for d in range(2):
        gza_copy(4, d, True).wait_recv()
    gxa_copy(4).start()
    keep_a(4, xh).start()
    for d in range(2):
        gzb_copy(3, d, True).wait_recv()
        gzb_copy(4, d).start()
        keep_bs(3 * (1, -1)[d])

    early, late = (0, 1, -1, 2, -2), (3, -3, 4)
    for k in early:
        take_gx(k)
    ig_rows(early)

    @pl.loop(1, 8)
    def _(j):
        for p in range(2):
            tok_copy(p, j).wait_send()

    @pl.loop(0, 8)
    def _(j):
        for p in range(2):
            fwd_copy(p, j).wait_send()
            xa_copy(j, p).wait_send()

    ring_a.drain()
    ring_b.drain()

    for k in late:
        take_gx(k)
    for d in range(2):
        gzb_copy(4, d, True).wait_recv()
    keep_bs(4)
    ig_rows(late)

    def ig_copy(j):
        return remote(ig_s.at[chip(j)], ig_r.at[j], ig_ss.at[j], ig_rs.at[j], peer(j))

    @pl.loop(1, 9)
    def _(j):
        d = chip(j)
        sib_copy(d).wait_recv()
        v = ig_acc[d, core] + sib_r[d].astype(F32)
        ig_acc[d, core] = v
        ig_s[d] = v.astype(BF16)

        @pl.when(j < 8)
        def _():
            ig_copy(j).start()

    @pl.loop(0, 8)
    def _(j):
        gxa_copy(j).wait_send()
        sib_copy(j).wait_send()

    for d in range(2):
        for step in range(1, 5):
            gza_copy(step, d).wait_send()
            gzb_copy(step, d).wait_send()
    gxb_copy(xh).wait_send()

    @pl.loop(1, 8)
    def _(j):
        ig_copy(j).wait()
        ig_acc[q, core] += ig_r[j].astype(F32)

    last = pltpu.make_async_copy(ig_acc.at[q, core], ig_out, lsem.at[1])
    last.start()

    @pl.loop(0, 8)
    def _(k):
        for x in range(2):
            keep_a(k, x).wait()
            keep_b(k, x).wait()

    keep_panel.wait()
    last.wait()


def weight_grads(d_in, panel, ig_in, ig_out, gg_out, ug_out, dg_out):
    gg_out[...] = dot(panel[0], d_in[1], 0, 0).astype(BF16)
    ug_out[...] = dot(panel[0], d_in[2], 0, 0).astype(BF16)
    dg_out[...] = dot(d_in[0], panel[1], 0, 0).astype(BF16)

    @pl.when(pl.program_id(0) == 0)
    def _():
        ig_out[...] = ig_in[...].astype(BF16)


def per_device(tokens, out_grad, gate_weight, up_weight, down_weight, cap_codes):
    hidden = gate_weight.shape[1]
    n = hidden // TILE
    na = 4
    nb = n - na
    wa, wb = na * TILE, nb * TILE
    dma = pltpu.SemaphoreType.DMA
    sh = jax.ShapeDtypeStruct
    scratch = [
        pltpu.VMEM((512, hidden), BF16),
        pltpu.VMEM((512, hidden), BF16),
        pltpu.VMEM((hidden, 512), BF16),
        pltpu.VMEM((2, NZ, 2, NB, 512), BF16),
        pltpu.VMEM((NZ, 3, NB, wa), F32),
        pltpu.VMEM((NZ, 6, NB, wb), F32),
        pltpu.VMEM((NZ, 3, NB, wa), BF16),
        pltpu.VMEM((NZ, 3, NB, wa), BF16),
        pltpu.VMEM((2, 4, 3, NB, wa), BF16),
        pltpu.VMEM((2, 4, 3, NB, wa), BF16),
        pltpu.VMEM((2, 4, 6, NB, wb), BF16),
        pltpu.VMEM((2, 4, 6, NB, wb), BF16),
        pltpu.VMEM((3, NB, wb), BF16),
        pltpu.VMEM((3, NB, wb), BF16),
        pltpu.VMEM((NZ, 2, 3, NB, wa), BF16),
        pltpu.VMEM((NZ, 6, NB, wb), BF16),
        pltpu.VMEM((NZ, 2, NB, 512), F32),
        pltpu.VMEM((NZ, NB, 512), BF16),
        pltpu.VMEM((NZ, NB, 512), BF16),
        pltpu.VMEM((NZ, NB, 512), BF16),
        pltpu.VMEM((NZ, NB, 512), BF16),
        dma((5,)), dma((2, NZ, 2)),
        dma((2, 8)), dma((2, 8)),
        dma((2, 8)), dma((2, 8)),
        dma((2, NZ)), dma((2, NZ)),
        dma((2, 4)), dma((2, 4)),
        dma((2, 4)), dma((2, 4)),
        dma, dma,
        dma((NZ,)), dma((NZ,)),
        dma((2, 4)), dma((2, 4)),
        dma((2, 4)), dma((2, 4)),
        dma, dma,
        dma((NZ,)), dma((NZ,)),
        dma((NZ,)), dma((NZ,)),
    ]
    any_spec = pl.BlockSpec(memory_space=pl.ANY)
    deltas, panel, ig_sum = pl.pallas_call(
        functools.partial(kernel, na, nb),
        out_shape=(sh((3, 512, hidden), BF16), sh((2, NZ, 2, NB, 512), BF16), sh((NB, 512), F32)),
        in_specs=[any_spec] * 5 + [pl.BlockSpec(memory_space=pltpu.VMEM)],
        out_specs=[any_spec] * 3,
        scratch_shapes=scratch,
        compiler_params=pltpu.CompilerParams(
            collective_id=0, has_side_effects=True, vmem_limit_bytes=60 << 20
        ),
        name="exchange",
    )(tokens, out_grad, gate_weight, up_weight, down_weight, cap_codes.reshape(hidden // 128, 128))
    wide = pl.BlockSpec((512, TILE), lambda i: (0, i))
    input_grad, gate_grad, up_grad, down_grad = pl.pallas_call(
        weight_grads,
        grid=(n,),
        out_shape=(
            sh((NB, 512), BF16),
            sh((512, hidden), BF16),
            sh((512, hidden), BF16),
            sh((hidden, 512), BF16),
        ),
        in_specs=[
            pl.BlockSpec((3, 512, TILE), lambda i: (0, 0, i)),
            pl.BlockSpec((2, 512, 512), lambda i: (0, 0, 0)),
            pl.BlockSpec((NB, 512), lambda i: (0, 0)),
        ],
        out_specs=(
            pl.BlockSpec((NB, 512), lambda i: (0, 0)),
            wide,
            wide,
            pl.BlockSpec((TILE, 512), lambda i: (i, 0)),
        ),
        compiler_params=pltpu.CompilerParams(vmem_limit_bytes=60 << 20),
        name="weight_grads",
    )(deltas, panel.reshape(2, 512, 512), ig_sum)
    return (input_grad, gate_grad, up_grad, down_grad)


def solution(mesh):
    return jax.shard_map(
        per_device,
        mesh=mesh,
        in_specs=(
            P("hid", "wid"),
            P("hid", "wid"),
            P("wid", "hid"),
            P("wid", "hid"),
            P("hid", "wid"),
            P("hid"),
        ),
        out_specs=(P("hid", "wid"), P("wid", "hid"), P("wid", "hid"), P("hid", "wid")),
        check_vma=False,
    )
```

time: 800 us -> 129 us (0.16); the launches traced: 789 us -> 127 us
  waiting for transfers between devices: 692 us -> 0 us
  Pallas kernels: 0 us -> 126 us
  blocking collectives: 37.1 us -> 0 us
  matrix products: 26.5 us -> 0 us
  between operations: 14.1 us -> 0.64 us
  local copies, waits for them, and re-layouts: 9.31 us -> 0 us
  other arithmetic: 9.25 us -> 0 us
    reduce_scatter x3 -> x0, waiting for transfers between devices: 465 us -> none  [the longest x1 213 us: per_device(): lax.psum_scatter(contract_last(rows_in, down_weight), 'wid', scatter_dime...]
    all_gather x3 -> x0, waiting for transfers between devices: 226 us -> none  [the longest x1 82.5 us: per_device(): lax.all_gather(gate_delta, 'wid', axis=0, tiled=True)]
    pallas_call x0 -> x2, Pallas kernels: none -> 126 us  [the longest x1 117 us: per_device(): pl.pallas_call(functools.partial(kernel, na, nb), out_shape=(sh((3, 512,...]
    all_gather x2 -> x0, blocking collectives: 37.1 us -> none  [the longest x1 18.7 us: per_device(): lax.all_gather(tokens, 'hid', axis=0, tiled=True)]
    dot_general x8 -> x0, matrix products: 26.5 us -> none  [the longest x3 12.6 us: contract_last(): lax.dot_general(left, right, (((1,), (1,)), ((), ())), preferred_element_...]
    unnamed x10 -> x0, local copies, waits for them, and re-layouts: 9.31 us -> none
  transfers between devices with their start and end apart: 6 -> 0, of which waited for: 6 -> 0; matrix products, arithmetic and copies ran while one was open for 4% -> 0% of each run, Pallas kernels for 0% -> 0%
where the time goes in v1:
time: 129 us; the launch traced here: 127 us
  Pallas kernels  126 us (98%)
    pallas_call x1, Pallas kernels, per_device(): pl.pallas_call(functools.partial(kernel, na, nb), out_shape=(sh((3, 512,...  117 us
    pallas_call x1, Pallas kernels, per_device(): pl.pallas_call(weight_grads, grid=(n,), out_shape=(sh((NB, 512), BF16), s...  9.23 us

profile of v1, /device:TPU:17, one launch (start us, length us, event | category | flops | bytes accessed | tf_op | source)
XLA Modules:
  0.0 126.9 jit_solution(3264883628179423216)
XLA Ops:
  0.6 117.0 %exchange.1 = (bf16[3,512,1792]{2,1,0:T(8,128)(2,1)}, bf16[2,8,2,32,512]{4,3,2,1,0:T(8,128)(2,1)}, f32[32,512]{1,0:T(8,128)}) custom-call(bf16[32,512]{1,0:T(8,128)(2,1)} %tok_in.1, bf16[32,512]{1,0:T(8,128)(2,1)} %og_in.1, bf16[512,1792]{1,0:T(8,128)(2,1)} %gw_in.1, bf16[512,1792]{1,0:T(8,128)(2,1)} %uw_in.1, bf16[1792,512]{1,0:T(8,128)(2,1)} %dw_in.1, ...), custom_call_target="tpu_custom_call" | custom-call | tf_op jit(solution)/shard_map/exchange/pallas_call | solution.py:480
  117.7 9.2 %weight_grads.1 = (bf16[32,512]{1,0:T(8,128)(2,1)}, bf16[512,1792]{1,0:T(8,128)(2,1)}, bf16[512,1792]{1,0:T(8,128)(2,1)}, bf16[1792,512]{1,0:T(8,128)(2,1)}) custom-call(bf16[3,512,1792]{2,1,0:T(8,128)(2,1)} %get-tuple-element.7.d_in, bf16[2,512,512]{2,1,0:T(8,128)(2,1)} %bitcast.2, f32[32,512]{1,0:T(8,128)} %get-tuple-element.9.ig_in), custom_call_target="tpu_custom_call" | custom-call | tf_op jit(solution)/shard_map/weight_grads/pallas_call | solution.py:492

commit v2 on v1

v2 whole, which is shorter than its diff:
```python
import functools

import jax
import jax.numpy as jnp
from jax import lax
from jax.experimental import pallas as pl
from jax.experimental.pallas import tpu as pltpu
from jax.sharding import PartitionSpec as P

MESH = pl.DeviceIdType.MESH
BF16 = jnp.bfloat16
F32 = jnp.float32

TILE = 256
NB = 32
NZ = 8
SCALE = 2.0**18


def dot(a, b, ca, cb):
    return lax.dot_general(a, b, (((ca,), (cb,)), ((), ())), preferred_element_type=F32)


def enc(v):
    u = v * SCALE
    return ((u * jnp.abs(u)) * (u * u)).astype(BF16)


def dec(y):
    y = y.astype(F32)
    root = lax.rsqrt(lax.rsqrt(jnp.maximum(jnp.abs(y), 2e-38)))
    return root * jnp.where(y < 0.0, -1.0 / SCALE, 1.0 / SCALE)


def kernel(
    na, nb,
    tok_in, og_in, gw_in, uw_in, dw_in, cap_in,
    d_out, panel_out, ig_out,
    gw, uw, dw, panel,
    pa, pb, xa_s, xa_r, sa, ra, sb, rb, xb_s, xb_r,
    ga, gb, ig_acc, sib_s, sib_r, ig_s, ig_r,
    lsem, dsem, tok_ss, tok_rs, fwd_ss, fwd_rs, xa_ss, xa_rs, za_ss, za_rs, zb_ss, zb_rs, xb_ss, xb_rs,
    gxa_ss, gxa_rs, gza_ss, gza_rs, gzb_ss, gzb_rs, gzb1_rs, gxb_ss, gxb_rs, sib_ss, sib_rs, ig_ss, ig_rs,
):
    wa, wb = na * TILE, nb * TILE
    h, w = lax.axis_index("hid"), lax.axis_index("wid")
    z, xh = w // 2, w % 2
    xo = 1 - xh
    q, core = h // 2, h % 2
    zp = lambda k: (z + k + NZ) % NZ
    up_dev, dn_dev, x_dev = (h, zp(1) * 2 + xh), (h, zp(-1) * 2 + xh), (h, z * 2 + xo)
    z_dev = (dn_dev, up_dev)
    sib_dev = (q * 2 + 1 - core, w)
    chip = lambda j: (q + j + 8) % 8
    peer = lambda j: (chip(j) * 2 + core, w)

    def remote(src, dst, ss, rs, dev):
        return pltpu.make_async_remote_copy(
            src_ref=src, dst_ref=dst, send_sem=ss, recv_sem=rs, device_id=dev, device_id_type=MESH
        )

    loads = [
        pltpu.make_async_copy(tok_in, panel.at[0, q, core], lsem.at[0]),
        pltpu.make_async_copy(og_in, panel.at[1, q, core], lsem.at[1]),
        pltpu.make_async_copy(gw_in, gw, lsem.at[2]),
        pltpu.make_async_copy(uw_in, uw, lsem.at[3]),
        pltpu.make_async_copy(dw_in, dw, lsem.at[4]),
    ]
    for c in loads:
        c.start()

    bar = pltpu.get_barrier_semaphore()
    for dev in (up_dev, dn_dev, x_dev, sib_dev):
        pl.semaphore_signal(bar, inc=1, device_id=dev, device_id_type=MESH)
    for j in range(1, 8):
        pl.semaphore_signal(bar, inc=1, device_id=peer(j), device_id_type=MESH)
    pl.semaphore_wait(bar, 11)

    def tok_copy(p, j):
        mine = panel.at[p, q, core]
        return remote(mine, mine, tok_ss, tok_rs.at[p, j], peer(j))

    def fwd_copy(p, j):
        blk = panel.at[p, chip(-j), core]
        return remote(blk, blk, fwd_ss, fwd_rs.at[p, j], sib_dev)

    def fwd_got(p, j):
        blk = panel.at[p, chip(-j), 1 - core]
        return remote(blk, blk, fwd_ss, fwd_rs.at[p, j], sib_dev)

    def send(p):
        loads[p].wait()

        @pl.loop(1, 8)
        def _(j):
            tok_copy(p, j).start()

        fwd_copy(p, 0).start()

    def forward(p):
        @pl.loop(1, 8)
        def _(j):
            tok_copy(p, j).wait_recv()
            fwd_copy(p, j).start()

    def gathered(p):
        @pl.loop(0, 8)
        def _(j):
            fwd_got(p, j).wait_recv()

    def partial(m, rows, col):
        if m == 2:
            return dot(rows, dw[pl.ds(col, TILE), :], 1, 1)
        return dot(rows, (gw, uw)[m][:, pl.ds(col, TILE)], 1, 0)

    def tile(i):
        return pl.ds(i * TILE, TILE)

    def part_a(ms, dst, x, f):
        for m in ms:
            rows = panel[m // 2, :, x].reshape(NZ * NB, 512)
            for i in range(na):
                dst[:, m, :, tile(i)] = f(partial(m, rows, i * TILE)).reshape(NZ, NB, TILE)

    def part_b(ms):
        for m in ms:
            rows = panel[m // 2].reshape(2 * NZ * NB, 512)
            for i in range(nb):
                v = partial(m, rows, wa + i * TILE).reshape(NZ, 2, NB, TILE)
                for x in range(2):
                    pb[:, 3 * x + m, :, tile(i)] = v[:, x]

    def xa_copy(k, g):
        d = zp(k)
        ms = (pl.ds(0, 2), pl.ds(2, 1))[g]
        return remote(xa_s.at[d, ms], xa_r.at[d, ms], xa_ss, xa_rs.at[g, d], x_dev)

    order = (4, 3, -3, 2, -2, 1, -1, 0)
    send(0)
    send(1)
    forward(0)
    forward(1)
    gathered(0)
    loads[2].wait()
    loads[3].wait()
    part_a((0, 1), xa_s, xo, enc)
    for k in order[:2]:
        xa_copy(k, 0).start()
    part_b((0, 1))
    gathered(1)
    loads[4].wait()
    part_a((2,), xa_s, xo, enc)
    for k in order[:2]:
        xa_copy(k, 1).start()
    for k in order[2:]:
        for g in range(2):
            xa_copy(k, g).start()
    part_b((2,))

    def hop(dst, own, recv, lo, hi):
        width = own.shape[-1] // 2

        @pl.loop(0, own.shape[0])
        def _(m):
            for i in range(lo, hi):
                c = pl.ds(i * width, width)
                v = own[m, :, c]
                for r in recv:
                    v = v + dec(r[m, :, c])
                dst[m, :, c] = enc(v) if dst.dtype == BF16 else v

    class Ring:
        def __init__(self, own, s, r, ss, rs):
            self.own, self.s, self.r, self.ss, self.rs = own, s, r, ss, rs
            self.half = own.shape[-1] // 2

        def copy(self, step, d):
            src, dst = self.s.at[d, step - 1], self.r.at[d, step - 1]
            if step == 1:
                c = pl.ds(d * self.half, self.half)
                src, dst = src.at[:, :, c], dst.at[:, :, c]
            return remote(src, dst, self.ss.at[min(step - 1, 1)], self.rs.at[d, step - 1], z_dev[d])

        def step(self, step):
            for d in range(2):
                own = self.own.at[zp((5 - step) * (-1, 1)[d])]
                src = self.s.at[d, step - 1]
                if step == 1:
                    hop(src, own, (), d, d + 1)
                else:
                    self.copy(step - 1, d).wait_recv()
                    got = self.r.at[d, step - 2]
                    if step == 2:
                        hop(src, own, (got,), d, d + 1)
                        hop(src, own, (), 1 - d, 2 - d)
                    else:
                        hop(src, own, (got,), 0, 2)
                self.copy(step, d).start()

        def finish(self, dst):
            for d in range(2):
                self.copy(4, d).wait_recv()
            hop(dst, self.own.at[z], (self.r.at[0, 3], self.r.at[1, 3]), 0, 2)

        def drain(self):
            one, rest = self.s.at[0, 0], self.s.at[:, pl.ds(1, 3)]
            remote(one, one, self.ss.at[0], self.rs.at[0, 0], z_dev[0]).wait_send()
            remote(rest, rest, self.ss.at[1], self.rs.at[0, 0], z_dev[0]).wait_send()

    ring_a = Ring(pa, sa, ra, za_ss, za_rs)
    ring_b = Ring(pb, sb, rb, zb_ss, zb_rs)

    ring_b.step(1)
    part_a((0, 1, 2), pa, xh, lambda v: v)

    def take_x(k):
        for g in range(2):
            xa_copy(k, g).wait_recv()
        d = zp(k)
        hop(pa.at[d], pa.at[d], (xa_r.at[d],), 0, 2)

    ring_b.step(2)
    take_x(4)
    ring_a.step(1)
    for s, ks in ((2, (3, -3)), (3, (2, -2))):
        ring_b.step(s + 1)
        for k in ks:
            take_x(k)
        ring_a.step(s)
    ring_b.finish(pb.at[z])
    hop(xb_s, pb.at[z, pl.ds(3 * xo, 3)], (), 0, 2)
    xb_copy = remote(xb_s, xb_r, xb_ss, xb_rs, x_dev)
    xb_copy.start()
    for k in (1, -1):
        take_x(k)
    ring_a.step(4)
    take_x(0)

    def local(src, dst, n, base):
        for i in range(n):
            gate, up, cap_grad = src[0, :, tile(i)], src[1, :, tile(i)], src[2, :, tile(i)]
            at = 2 * (base + i)
            codes = jnp.concatenate([cap_in[at : at + 1, :], cap_in[at + 1 : at + 2, :]], axis=1)
            cap = codes.astype(F32) * (1.0 / 512.0)
            sig = 1.0 / (1.0 + jnp.exp(-gate))
            act = gate * sig
            squash = jnp.tanh(act * up / cap)
            hid_grad = cap_grad * (1.0 - squash * squash)
            dst[0, :, tile(i)] = (cap * squash).astype(BF16)
            dst[1, :, tile(i)] = (hid_grad * up * sig * (1.0 + gate * (1.0 - sig))).astype(BF16)
            dst[2, :, tile(i)] = (hid_grad * act).astype(BF16)

    xb_copy.wait()
    own_b = pb.at[z, pl.ds(3 * xh, 3)]
    hop(own_b, own_b, (xb_r,), 0, 2)
    local(own_b, gb.at[z, pl.ds(3 * xh, 3)], nb, na)

    def gxb_copy(x):
        blk = gb.at[z, pl.ds(3 * x, 3)]
        return remote(blk, blk, gxb_ss, gxb_rs, x_dev)

    gxb_copy(xh).start()
    ring_a.finish(pa.at[z])
    local(pa.at[z], ga.at[z, xh], na, 0)

    def halves(blk, step, d, width):
        return blk.at[:, :, pl.ds(d * (width // 2), width // 2)] if step == 4 else blk

    def gza_copy(step, d, got=False):
        blk = halves(ga.at[zp((step if got else step - 1) * (1, -1)[d]), xh], step, d, wa)
        return remote(blk, blk, gza_ss.at[step // 4], gza_rs.at[d, step - 1], z_dev[d])

    def gxa_copy(k, got=False):
        blk = ga.at[zp(k), xo if got else xh]
        return remote(blk, blk, gxa_ss, gxa_rs.at[zp(k)], x_dev)

    def gzb_copy(step, d, got=False):
        blk = halves(gb.at[zp((step if got else step - 1) * (1, -1)[d])], step, d, wb)
        return remote(blk, blk, gzb_ss.at[step // 4], gzb_rs.at[d, step - 1], z_dev[d])

    def gzb_first(d, x, got=False):
        blk = gb.at[zp((1, -1)[d] if got else 0), pl.ds(3 * x, 3)]
        return remote(blk, blk, gzb_ss.at[0], gzb1_rs.at[d, x], z_dev[d])

    def keep_a(k, x):
        d = zp(k)
        t = pl.multiple_of((d * 2 + x) * NB, NB)
        return pltpu.make_async_copy(ga.at[d, x], d_out.at[:, pl.ds(t, NB), pl.ds(0, wa)], dsem.at[0])

    def keep_b(k, x):
        d = zp(k)
        t = pl.multiple_of((d * 2 + x) * NB, NB)
        return pltpu.make_async_copy(
            gb.at[d, pl.ds(3 * x, 3)], d_out.at[:, pl.ds(t, NB), pl.ds(wa, wb)], dsem.at[1]
        )

    def keep_bs(k):
        for x in range(2):
            keep_b(k, x).start()

    for d in range(2):
        gza_copy(1, d).start()
    gxa_copy(0).start()
    for d in range(2):
        gzb_first(d, xh).start()
    keep_a(0, xh).start()
    keep_panel = pltpu.make_async_copy(panel, panel_out, lsem.at[0])
    keep_panel.start()

    def ig_rows(ks):
        def rows(ref):
            return jnp.concatenate([ref(zp(k), x) for k in ks for x in range(2)], axis=0)

        v = 0.0
        for m, wt in ((1, gw), (2, uw)):
            v = v + dot(rows(lambda d, x: ga[d, x, m]), wt[:, :wa], 1, 1)
            v = v + dot(rows(lambda d, x: gb[d, 3 * x + m]), wt[:, wa:], 1, 1)
        for n_k, k in enumerate(ks):
            ig_acc[zp(k)] = v[n_k * 2 * NB : (n_k + 1) * 2 * NB].reshape(2, NB, 512)
        for k in ks:
            d = zp(k)
            sib_s[d] = ig_acc[d, 1 - core].astype(BF16)
            sib_copy(d).start()

    def ig_send(ks):
        for k in ks:
            d = zp(k)
            sib_copy(d).wait_recv()
            v = ig_acc[d, core] + sib_r[d].astype(F32)
            ig_acc[d, core] = v
            ig_s[d] = v.astype(BF16)

            @pl.when(d != q)
            def _():
                ig_copy((d - q + 8) % 8).start()

    def ig_copy(j):
        return remote(ig_s.at[chip(j)], ig_r.at[j], ig_ss, ig_rs.at[j], peer(j))

    def sib_copy(d):
        return remote(sib_s.at[d], sib_r.at[d], sib_ss, sib_rs.at[d], sib_dev)

    def take_gx(k):
        gxa_copy(k, True).wait_recv()
        keep_a(k, xo).start()

    def forward_a(step):
        for d in range(2):
            k = (step - 1) * (1, -1)[d]
            gza_copy(step - 1, d, True).wait_recv()
            gza_copy(step, d).start()
            gxa_copy(k).start()
            keep_a(k, xh).start()

    def forward_b(step):
        for d in range(2):
            if step == 2:
                for x in range(2):
                    gzb_first(d, x, True).wait_recv()
            else:
                gzb_copy(step - 1, d, True).wait_recv()
            gzb_copy(step, d).start()
            keep_bs((step - 1) * (1, -1)[d])

    forward_a(2)
    gxb_copy(xo).wait_recv()
    for d in range(2):
        gzb_first(d, xo).start()
    keep_bs(0)
    forward_a(3)
    forward_b(2)
    forward_a(4)
    forward_b(3)

    def sent(ref, sem):
        remote(ref, ref, sem, gxb_rs, x_dev).wait_send()

    sent(panel.at[0, pl.ds(0, 7)], tok_ss)
    sent(panel.at[0], fwd_ss)
    sent(xa_s, xa_ss)
    ring_a.drain()
    ring_b.drain()
    early = (0, 1, -1, 2, -2)
    for k in early:
        take_gx(k)
    ig_rows(early)
    for d in range(2):
        gza_copy(4, d, True).wait_recv()
    gxa_copy(4).start()
    keep_a(4, xh).start()
    ig_send(early)
    forward_b(4)
    for k in (3, -3):
        take_gx(k)
    ig_rows((3, -3))
    ig_send((3, -3))
    take_gx(4)
    for d in range(2):
        gzb_copy(4, d, True).wait_recv()
    keep_bs(4)
    ig_rows((4,))
    ig_send((4,))

    sent(xa_s, gxa_ss)
    sent(sib_s, sib_ss)
    sent(sa.at[0, 0], gza_ss.at[1])
    sent(sa.at[:, pl.ds(0, 3)], gza_ss.at[0])
    sent(sb.at[0, 0], gzb_ss.at[1])
    sent(sb.at[:, pl.ds(0, 3)], gzb_ss.at[0])
    gxb_copy(xh).wait_send()

    @pl.loop(1, 8)
    def _(j):
        ig_copy(j).wait_recv()
        ig_acc[q, core] += ig_r[j].astype(F32)

    sent(ig_s.at[pl.ds(0, 7)], ig_ss)
    last = pltpu.make_async_copy(ig_acc.at[q, core], ig_out, lsem.at[1])
    last.start()

    pltpu.make_async_copy(ga, ga, dsem.at[0]).wait()
    pltpu.make_async_copy(gb, gb, dsem.at[1]).wait()
    keep_panel.wait()
    last.wait()


def weight_grads(d_in, panel_in, ig_in, ig_out, gg_out, ug_out, dg_out, d, panel, gg, ug, dg, isem, osem):
    loads = {}
    for at, (src, dst) in enumerate(
        (
            (panel_in.at[0], panel.at[0]),
            (d_in.at[1], d.at[1]),
            (d_in.at[2], d.at[2]),
            (panel_in.at[1], panel.at[1]),
            (d_in.at[0], d.at[0]),
        )
    ):
        loads[at] = pltpu.make_async_copy(src, dst, isem.at[at])
        loads[at].start()
    ig_out[...] = ig_in[...].astype(BF16)
    n = d.shape[2] // TILE
    stores = []

    def store(src, dst):
        stores.append(pltpu.make_async_copy(src, dst, osem.at[len(stores)]))
        stores[-1].start()

    loads[0].wait()
    for m, dst, out in ((1, gg, gg_out), (2, ug, ug_out)):
        loads[m].wait()
        for i in range(n):
            c = pl.ds(i * TILE, TILE)
            dst[:, c] = dot(panel[0], d[m, :, c], 0, 0).astype(BF16)
        store(dst, out)
    loads[3].wait()
    loads[4].wait()
    for lo, hi in ((0, 4), (4, 6), (6, 7)):
        for i in range(lo, hi):
            c = pl.ds(i * TILE, TILE)
            dg[c, :] = dot(d[0, :, c], panel[1], 0, 0).astype(BF16)
        rows = pl.ds(lo * TILE, (hi - lo) * TILE)
        store(dg.at[rows], dg_out.at[rows])
    for c in stores:
        c.wait()


def per_device(tokens, out_grad, gate_weight, up_weight, down_weight, cap_codes):
    hidden = gate_weight.shape[1]
    n = hidden // TILE
    na = 4
    nb = n - na
    wa, wb = na * TILE, nb * TILE
    dma = pltpu.SemaphoreType.DMA
    sh = jax.ShapeDtypeStruct
    scratch = [
        pltpu.VMEM((512, hidden), BF16),
        pltpu.VMEM((512, hidden), BF16),
        pltpu.VMEM((hidden, 512), BF16),
        pltpu.VMEM((2, NZ, 2, NB, 512), BF16),
        pltpu.VMEM((NZ, 3, NB, wa), F32),
        pltpu.VMEM((NZ, 6, NB, wb), F32),
        pltpu.VMEM((NZ, 3, NB, wa), BF16),
        pltpu.VMEM((NZ, 3, NB, wa), BF16),
        pltpu.VMEM((2, 4, 3, NB, wa), BF16),
        pltpu.VMEM((2, 4, 3, NB, wa), BF16),
        pltpu.VMEM((2, 4, 6, NB, wb), BF16),
        pltpu.VMEM((2, 4, 6, NB, wb), BF16),
        pltpu.VMEM((3, NB, wb), BF16),
        pltpu.VMEM((3, NB, wb), BF16),
        pltpu.VMEM((NZ, 2, 3, NB, wa), BF16),
        pltpu.VMEM((NZ, 6, NB, wb), BF16),
        pltpu.VMEM((NZ, 2, NB, 512), F32),
        pltpu.VMEM((NZ, NB, 512), BF16),
        pltpu.VMEM((NZ, NB, 512), BF16),
        pltpu.VMEM((NZ, NB, 512), BF16),
        pltpu.VMEM((NZ, NB, 512), BF16),
        dma((5,)), dma((2,)),
        dma, dma((2, 8)),
        dma, dma((2, 8)),
        dma, dma((2, NZ)),
        dma((2,)), dma((2, 4)),
        dma((2,)), dma((2, 4)),
        dma, dma,
        dma, dma((NZ,)),
        dma((2,)), dma((2, 4)),
        dma((2,)), dma((2, 4)), dma((2, 2)),
        dma, dma,
        dma, dma((NZ,)),
        dma, dma((NZ,)),
    ]
    any_spec = pl.BlockSpec(memory_space=pl.ANY)
    deltas, panel, ig_sum = pl.pallas_call(
        functools.partial(kernel, na, nb),
        out_shape=(sh((3, 512, hidden), BF16), sh((2, NZ, 2, NB, 512), BF16), sh((NB, 512), F32)),
        in_specs=[any_spec] * 5 + [pl.BlockSpec(memory_space=pltpu.VMEM)],
        out_specs=[any_spec] * 3,
        scratch_shapes=scratch,
        compiler_params=pltpu.CompilerParams(
            collective_id=0, has_side_effects=True, vmem_limit_bytes=60 << 20
        ),
        name="exchange",
    )(tokens, out_grad, gate_weight, up_weight, down_weight, cap_codes.reshape(hidden // 128, 128))
    return pl.pallas_call(
        weight_grads,
        out_shape=(
            sh((NB, 512), BF16),
            sh((512, hidden), BF16),
            sh((512, hidden), BF16),
            sh((hidden, 512), BF16),
        ),
        in_specs=[any_spec, any_spec, pl.BlockSpec(memory_space=pltpu.VMEM)],
        out_specs=(pl.BlockSpec(memory_space=pltpu.VMEM), any_spec, any_spec, any_spec),
        scratch_shapes=[
            pltpu.VMEM((3, 512, hidden), BF16),
            pltpu.VMEM((2, 512, 512), BF16),
            pltpu.VMEM((512, hidden), BF16),
            pltpu.VMEM((512, hidden), BF16),
            pltpu.VMEM((hidden, 512), BF16),
            dma((5,)),
            dma((5,)),
        ],
        compiler_params=pltpu.CompilerParams(vmem_limit_bytes=60 << 20),
        name="weight_grads",
    )(deltas, panel.reshape(2, 512, 512), ig_sum)


def solution(mesh):
    return jax.shard_map(
        per_device,
        mesh=mesh,
        in_specs=(
            P("hid", "wid"),
            P("hid", "wid"),
            P("wid", "hid"),
            P("wid", "hid"),
            P("hid", "wid"),
            P("hid"),
        ),
        out_specs=(P("hid", "wid"), P("wid", "hid"), P("wid", "hid"), P("hid", "wid")),
        check_vma=False,
    )
```

time: 129 us -> 119 us (0.922)
  Pallas kernels: 126 us -> 117 us
    pallas_call x1, Pallas kernels: 117 us -> 109 us  [per_device(): pl.pallas_call(functools.partial(kernel, na, nb), out_shape=(sh((3, 512,...]
    pallas_call x1, Pallas kernels: 9.23 us -> 7.71 us  [per_device(): pl.pallas_call(weight_grads, out_shape=(sh((NB, 512), BF16), sh((512, hid...]
where the time goes in v2:
time: 119 us; the launch traced here: 118 us
  Pallas kernels  117 us (98%)
    pallas_call x1, Pallas kernels, per_device(): pl.pallas_call(functools.partial(kernel, na, nb), out_shape=(sh((3, 512,...  109 us
    pallas_call x1, Pallas kernels, per_device(): pl.pallas_call(weight_grads, out_shape=(sh((NB, 512), BF16), sh((512, hid...  7.71 us

profile of v2, /device:TPU:17, one launch (start us, length us, event | category | flops | bytes accessed | tf_op | source)
XLA Modules:
  0.0 117.5 jit_solution(1405592496873361467)
XLA Ops:
  0.6 109.2 %exchange.1 = (bf16[3,512,1792]{2,1,0:T(8,128)(2,1)}, bf16[2,8,2,32,512]{4,3,2,1,0:T(8,128)(2,1)}, f32[32,512]{1,0:T(8,128)}) custom-call(bf16[32,512]{1,0:T(8,128)(2,1)} %tok_in.1, bf16[32,512]{1,0:T(8,128)(2,1)} %og_in.1, bf16[512,1792]{1,0:T(8,128)(2,1)} %gw_in.1, bf16[512,1792]{1,0:T(8,128)(2,1)} %uw_in.1, bf16[1792,512]{1,0:T(8,128)(2,1)} %dw_in.1, ...), custom_call_target="tpu_custom_call" | custom-call | tf_op jit(solution)/shard_map/exchange/pallas_call | solution.py:512
  109.8 7.7 %weight_grads.1 = (bf16[32,512]{1,0:T(8,128)(2,1)}, bf16[512,1792]{1,0:T(8,128)(2,1)}, bf16[512,1792]{1,0:T(8,128)(2,1)}, bf16[1792,512]{1,0:T(8,128)(2,1)}) custom-call(bf16[3,512,1792]{2,1,0:T(8,128)(2,1)} %get-tuple-element.7.d_in, bf16[2,512,512]{2,1,0:T(8,128)(2,1)} %bitcast.2, f32[32,512]{1,0:T(8,128)} %get-tuple-element.9.ig_in), custom_call_target="tpu_custom_call" | custom-call | tf_op jit(solution)/shard_map/weight_grads/pallas_call | solution.py:523

commit v3 on v2

--- a/solution.py
+++ b/solution.py
@@ -40,7 +40,7 @@
     pa, pb, xa_s, xa_r, sa, ra, sb, rb, xb_s, xb_r,
     ga, gb, ig_acc, sib_s, sib_r, ig_s, ig_r,
     lsem, dsem, tok_ss, tok_rs, fwd_ss, fwd_rs, xa_ss, xa_rs, za_ss, za_rs, zb_ss, zb_rs, xb_ss, xb_rs,
-    gxa_ss, gxa_rs, gza_ss, gza_rs, gzb_ss, gzb_rs, gzb1_rs, gxb_ss, gxb_rs, sib_ss, sib_rs, ig_ss, ig_rs,
+    gxa_ss, gxa_rs, gza_ss, gza_rs, gzb_ss, gzb_rs, gxb_ss, gxb_rs, sib_ss, sib_rs, ig_ss, ig_rs,
 ):
     wa, wb = na * TILE, nb * TILE
     h, w = lax.axis_index("hid"), lax.axis_index("wid")
@@ -139,7 +139,6 @@
     send(0)
     send(1)
     forward(0)
-    forward(1)
     gathered(0)
     loads[2].wait()
     loads[3].wait()
@@ -147,14 +146,9 @@
     for k in order[:2]:
         xa_copy(k, 0).start()
     part_b((0, 1))
+    forward(1)
     gathered(1)
     loads[4].wait()
-    part_a((2,), xa_s, xo, enc)
-    for k in order[:2]:
-        xa_copy(k, 1).start()
-    for k in order[2:]:
-        for g in range(2):
-            xa_copy(k, g).start()
     part_b((2,))
 
     def hop(dst, own, recv, lo, hi):
@@ -172,7 +166,7 @@
     class Ring:
         def __init__(self, own, s, r, ss, rs):
             self.own, self.s, self.r, self.ss, self.rs = own, s, r, ss, rs
-            self.half = own.shape[-1] // 2
+            self.half = s.shape[-1] // 2
 
         def copy(self, step, d):
             src, dst = self.s.at[d, step - 1], self.r.at[d, step - 1]
@@ -183,7 +177,7 @@
 
         def step(self, step):
             for d in range(2):
-                own = self.own.at[zp((5 - step) * (-1, 1)[d])]
+                own = self.own(zp((5 - step) * (-1, 1)[d]))
                 src = self.s.at[d, step - 1]
                 if step == 1:
                     hop(src, own, (), d, d + 1)
@@ -200,17 +194,39 @@
         def finish(self, dst):
             for d in range(2):
                 self.copy(4, d).wait_recv()
-            hop(dst, self.own.at[z], (self.r.at[0, 3], self.r.at[1, 3]), 0, 2)
+            hop(dst, self.own(z), (self.r.at[0, 3], self.r.at[1, 3]), 0, 2)
 
         def drain(self):
             one, rest = self.s.at[0, 0], self.s.at[:, pl.ds(1, 3)]
             remote(one, one, self.ss.at[0], self.rs.at[0, 0], z_dev[0]).wait_send()
             remote(rest, rest, self.ss.at[1], self.rs.at[0, 0], z_dev[0]).wait_send()
 
-    ring_a = Ring(pa, sa, ra, za_ss, za_rs)
-    ring_b = Ring(pb, sb, rb, zb_ss, zb_rs)
-
-    ring_b.step(1)
+    ha = wa // 2
+    cols_a = (pl.ds(0, ha), pl.ds(ha, ha))
+    xs = (xo, xh)
+    rings_a = [
+        Ring(lambda d, c=cols_a[i]: pa.at[d, :, :, c], sa.at[i], ra.at[i], za_ss.at[i], za_rs.at[i]) for i in range(2)
+    ]
+    rings_b = [
+        Ring(lambda d, x=xs[i]: pb.at[d, pl.ds(3 * x, 3)], sb.at[i], rb.at[i], zb_ss.at[i], zb_rs.at[i])
+        for i in range(2)
+    ]
+
+    def step_a(step):
+        for ring in rings_a:
+            ring.step(step)
+
+    def step_b(step):
+        for ring in rings_b:
+            ring.step(step)
+
+    step_b(1)
+    part_a((2,), xa_s, xo, enc)
+    for k in order[:2]:
+        xa_copy(k, 1).start()
+    for k in order[2:]:
+        for g in range(2):
+            xa_copy(k, g).start()
     part_a((0, 1, 2), pa, xh, lambda v: v)
 
     def take_x(k):
@@ -219,22 +235,23 @@
         d = zp(k)
         hop(pa.at[d], pa.at[d], (xa_r.at[d],), 0, 2)
 
-    ring_b.step(2)
+    step_b(2)
     take_x(4)
-    ring_a.step(1)
+    step_a(1)
     for s, ks in ((2, (3, -3)), (3, (2, -2))):
-        ring_b.step(s + 1)
+        step_b(s + 1)
         for k in ks:
             take_x(k)
-        ring_a.step(s)
-    ring_b.finish(pb.at[z])
-    hop(xb_s, pb.at[z, pl.ds(3 * xo, 3)], (), 0, 2)
+        step_a(s)
+    rings_b[0].finish(xb_s)
     xb_copy = remote(xb_s, xb_r, xb_ss, xb_rs, x_dev)
     xb_copy.start()
     for k in (1, -1):
         take_x(k)
-    ring_a.step(4)
+    step_a(4)
     take_x(0)
+    own_b = pb.at[z, pl.ds(3 * xh, 3)]
+    rings_b[1].finish(own_b)
 
     def local(src, dst, n, base):
         for i in range(n):
@@ -251,7 +268,6 @@
             dst[2, :, tile(i)] = (hid_grad * act).astype(BF16)
 
     xb_copy.wait()
-    own_b = pb.at[z, pl.ds(3 * xh, 3)]
     hop(own_b, own_b, (xb_r,), 0, 2)
     local(own_b, gb.at[z, pl.ds(3 * xh, 3)], nb, na)
 
@@ -260,27 +276,26 @@
         return remote(blk, blk, gxb_ss, gxb_rs, x_dev)
 
     gxb_copy(xh).start()
-    ring_a.finish(pa.at[z])
+    for i in range(2):
+        rings_a[i].finish(pa.at[z, :, :, cols_a[i]])
     local(pa.at[z], ga.at[z, xh], na, 0)
 
     def halves(blk, step, d, width):
         return blk.at[:, :, pl.ds(d * (width // 2), width // 2)] if step == 4 else blk
 
-    def gza_copy(step, d, got=False):
-        blk = halves(ga.at[zp((step if got else step - 1) * (1, -1)[d]), xh], step, d, wa)
-        return remote(blk, blk, gza_ss.at[step // 4], gza_rs.at[d, step - 1], z_dev[d])
-
-    def gxa_copy(k, got=False):
-        blk = ga.at[zp(k), xo if got else xh]
-        return remote(blk, blk, gxa_ss, gxa_rs.at[zp(k)], x_dev)
-
-    def gzb_copy(step, d, got=False):
-        blk = halves(gb.at[zp((step if got else step - 1) * (1, -1)[d])], step, d, wb)
-        return remote(blk, blk, gzb_ss.at[step // 4], gzb_rs.at[d, step - 1], z_dev[d])
-
-    def gzb_first(d, x, got=False):
-        blk = gb.at[zp((1, -1)[d] if got else 0), pl.ds(3 * x, 3)]
-        return remote(blk, blk, gzb_ss.at[0], gzb1_rs.at[d, x], z_dev[d])
+    def gza_copy(i, step, d, got=False):
+        blk = ga.at[zp((step if got else step - 1) * (1, -1)[d]), xh, :, :, cols_a[i]]
+        blk = halves(blk, step, d, ha)
+        return remote(blk, blk, gza_ss.at[step // 4], gza_rs.at[i, d, step - 1], z_dev[d])
+
+    def gxa_copy(i, k, got=False):
+        blk = ga.at[zp(k), xo if got else xh, :, :, cols_a[i]]
+        return remote(blk, blk, gxa_ss, gxa_rs.at[i, zp(k)], x_dev)
+
+    def gzb_copy(i, step, d, got=False):
+        blk = gb.at[zp((step if got else step - 1) * (1, -1)[d]), pl.ds(3 * xs[i], 3)]
+        blk = halves(blk, step, d, wb)
+        return remote(blk, blk, gzb_ss.at[step // 4], gzb_rs.at[i, d, step - 1], z_dev[d])
 
     def keep_a(k, x):
         d = zp(k)
@@ -298,25 +313,32 @@
         for x in range(2):
             keep_b(k, x).start()
 
+    for i in range(2):
+        for d in range(2):
+            gza_copy(i, 1, d).start()
     for d in range(2):
-        gza_copy(1, d).start()
-    gxa_copy(0).start()
-    for d in range(2):
-        gzb_first(d, xh).start()
+        gzb_copy(1, 1, d).start()
+    for i in range(2):
+        gxa_copy(i, 0).start()
     keep_a(0, xh).start()
     keep_panel = pltpu.make_async_copy(panel, panel_out, lsem.at[0])
     keep_panel.start()
 
-    def ig_rows(ks):
+    def ig_rows(ks, a=True, b=True):
         def rows(ref):
             return jnp.concatenate([ref(zp(k), x) for k in ks for x in range(2)], axis=0)
 
         v = 0.0
         for m, wt in ((1, gw), (2, uw)):
-            v = v + dot(rows(lambda d, x: ga[d, x, m]), wt[:, :wa], 1, 1)
-            v = v + dot(rows(lambda d, x: gb[d, 3 * x + m]), wt[:, wa:], 1, 1)
+            if a:
+                v = v + dot(rows(lambda d, x: ga[d, x, m]), wt[:, :wa], 1, 1)
+            if b:
+                v = v + dot(rows(lambda d, x: gb[d, 3 * x + m]), wt[:, wa:], 1, 1)
         for n_k, k in enumerate(ks):
-            ig_acc[zp(k)] = v[n_k * 2 * NB : (n_k + 1) * 2 * NB].reshape(2, NB, 512)
+            part = v[n_k * 2 * NB : (n_k + 1) * 2 * NB].reshape(2, NB, 512)
+            ig_acc[zp(k)] = part if a else ig_acc[zp(k)] + part
+        if not b:
+            return
         for k in ks:
             d = zp(k)
             sib_s[d] = ig_acc[d, 1 - core].astype(BF16)
@@ -341,36 +363,37 @@
         return remote(sib_s.at[d], sib_r.at[d], sib_ss, sib_rs.at[d], sib_dev)
 
     def take_gx(k):
-        gxa_copy(k, True).wait_recv()
+        for i in range(2):
+            gxa_copy(i, k, True).wait_recv()
         keep_a(k, xo).start()
 
     def forward_a(step):
+        for i in range(2):
+            for d in range(2):
+                k = (step - 1) * (1, -1)[d]
+                gza_copy(i, step - 1, d, True).wait_recv()
+                gza_copy(i, step, d).start()
+                gxa_copy(i, k).start()
+                if i == 1:
+                    keep_a(k, xh).start()
+
+    def forward_b(i, step):
         for d in range(2):
-            k = (step - 1) * (1, -1)[d]
-            gza_copy(step - 1, d, True).wait_recv()
-            gza_copy(step, d).start()
-            gxa_copy(k).start()
-            keep_a(k, xh).start()
-
-    def forward_b(step):
-        for d in range(2):
-            if step == 2:
-                for x in range(2):
-                    gzb_first(d, x, True).wait_recv()
-            else:
-                gzb_copy(step - 1, d, True).wait_recv()
-            gzb_copy(step, d).start()
-            keep_bs((step - 1) * (1, -1)[d])
+            gzb_copy(i, step - 1, d, True).wait_recv()
+            gzb_copy(i, step, d).start()
+            keep_b((step - 1) * (1, -1)[d], xs[i]).start()
 
     forward_a(2)
     gxb_copy(xo).wait_recv()
     for d in range(2):
-        gzb_first(d, xo).start()
+        gzb_copy(0, 1, d).start()
     keep_bs(0)
+    forward_b(1, 2)
     forward_a(3)
-    forward_b(2)
+    forward_b(0, 2)
     forward_a(4)
-    forward_b(3)
+    forward_b(1, 3)
+    forward_b(0, 3)
 
     def sent(ref, sem):
         remote(ref, ref, sem, gxb_rs, x_dev).wait_send()
@@ -378,35 +401,39 @@
     sent(panel.at[0, pl.ds(0, 7)], tok_ss)
     sent(panel.at[0], fwd_ss)
     sent(xa_s, xa_ss)
-    ring_a.drain()
-    ring_b.drain()
+    for ring in rings_a + rings_b:
+        ring.drain()
     early = (0, 1, -1, 2, -2)
     for k in early:
         take_gx(k)
     ig_rows(early)
-    for d in range(2):
-        gza_copy(4, d, True).wait_recv()
-    gxa_copy(4).start()
+    for i in range(2):
+        for d in range(2):
+            gza_copy(i, 4, d, True).wait_recv()
+        gxa_copy(i, 4).start()
     keep_a(4, xh).start()
+    forward_b(1, 4)
+    forward_b(0, 4)
     ig_send(early)
-    forward_b(4)
     for k in (3, -3):
         take_gx(k)
     ig_rows((3, -3))
     ig_send((3, -3))
     take_gx(4)
-    for d in range(2):
-        gzb_copy(4, d, True).wait_recv()
+    ig_rows((4,), b=False)
+    for i in (1, 0):
+        for d in range(2):
+            gzb_copy(i, 4, d, True).wait_recv()
     keep_bs(4)
-    ig_rows((4,))
+    ig_rows((4,), a=False)
     ig_send((4,))
 
     sent(xa_s, gxa_ss)
     sent(sib_s, sib_ss)
-    sent(sa.at[0, 0], gza_ss.at[1])
-    sent(sa.at[:, pl.ds(0, 3)], gza_ss.at[0])
-    sent(sb.at[0, 0], gzb_ss.at[1])
-    sent(sb.at[:, pl.ds(0, 3)], gzb_ss.at[0])
+    sent(sa.at[:, 0, 0], gza_ss.at[1])
+    sent(sa.at[:, :, pl.ds(0, 3)], gza_ss.at[0])
+    sent(sb.at[:, 0, 0], gzb_ss.at[1])
+    sent(sb.at[:, :, pl.ds(0, 3)], gzb_ss.at[0])
     gxb_copy(xh).wait_send()
 
     @pl.loop(1, 8)
@@ -424,20 +451,22 @@
     last.wait()
 
 
-def weight_grads(d_in, panel_in, ig_in, ig_out, gg_out, ug_out, dg_out, d, panel, gg, ug, dg, isem, osem):
-    loads = {}
-    for at, (src, dst) in enumerate(
-        (
-            (panel_in.at[0], panel.at[0]),
-            (d_in.at[1], d.at[1]),
-            (d_in.at[2], d.at[2]),
-            (panel_in.at[1], panel.at[1]),
-            (d_in.at[0], d.at[0]),
-        )
+def weight_grads(
+    d_in, panel_in, ig_in, ig_out, gg_out, ug_out, dg_out, d, panel, gg, ug, dg, ig_v, ig_b, isem, osem
+):
+    first, rest = pl.ds(0, 2 * TILE), pl.ds(2 * TILE, d.shape[2] - 2 * TILE)
+    loads = []
+    for src, dst in (
+        (panel_in.at[0], panel.at[0]),
+        (d_in.at[1, :, first], d.at[1, :, first]),
+        (d_in.at[1, :, rest], d.at[1, :, rest]),
+        (d_in.at[2], d.at[2]),
+        (panel_in.at[1], panel.at[1]),
+        (d_in.at[0], d.at[0]),
+        (ig_in, ig_v),
     ):
-        loads[at] = pltpu.make_async_copy(src, dst, isem.at[at])
-        loads[at].start()
-    ig_out[...] = ig_in[...].astype(BF16)
+        loads.append(pltpu.make_async_copy(src, dst, isem.at[len(loads)]))
+        loads[-1].start()
     n = d.shape[2] // TILE
     stores = []
 
@@ -446,14 +475,21 @@
         stores[-1].start()
 
     loads[0].wait()
+    loads[1].wait()
     for m, dst, out in ((1, gg, gg_out), (2, ug, ug_out)):
-        loads[m].wait()
         for i in range(n):
+            if (m, i) == (1, 2):
+                loads[2].wait()
+            if (m, i) == (2, 0):
+                loads[3].wait()
             c = pl.ds(i * TILE, TILE)
             dst[:, c] = dot(panel[0], d[m, :, c], 0, 0).astype(BF16)
         store(dst, out)
-    loads[3].wait()
+    loads[6].wait()
+    ig_b[...] = ig_v[...].astype(BF16)
+    store(ig_b, ig_out)
     loads[4].wait()
+    loads[5].wait()
     for lo, hi in ((0, 4), (4, 6), (6, 7)):
         for i in range(lo, hi):
             c = pl.ds(i * TILE, TILE)
@@ -481,10 +517,10 @@
         pltpu.VMEM((NZ, 6, NB, wb), F32),
         pltpu.VMEM((NZ, 3, NB, wa), BF16),
         pltpu.VMEM((NZ, 3, NB, wa), BF16),
-        pltpu.VMEM((2, 4, 3, NB, wa), BF16),
-        pltpu.VMEM((2, 4, 3, NB, wa), BF16),
-        pltpu.VMEM((2, 4, 6, NB, wb), BF16),
-        pltpu.VMEM((2, 4, 6, NB, wb), BF16),
+        pltpu.VMEM((2, 2, 4, 3, NB, wa // 2), BF16),
+        pltpu.VMEM((2, 2, 4, 3, NB, wa // 2), BF16),
+        pltpu.VMEM((2, 2, 4, 3, NB, wb), BF16),
+        pltpu.VMEM((2, 2, 4, 3, NB, wb), BF16),
         pltpu.VMEM((3, NB, wb), BF16),
         pltpu.VMEM((3, NB, wb), BF16),
         pltpu.VMEM((NZ, 2, 3, NB, wa), BF16),
@@ -498,12 +534,12 @@
         dma, dma((2, 8)),
         dma, dma((2, 8)),
         dma, dma((2, NZ)),
-        dma((2,)), dma((2, 4)),
-        dma((2,)), dma((2, 4)),
+        dma((2, 2)), dma((2, 2, 4)),
+        dma((2, 2)), dma((2, 2, 4)),
         dma, dma,
-        dma, dma((NZ,)),
-        dma((2,)), dma((2, 4)),
-        dma((2,)), dma((2, 4)), dma((2, 2)),
+        dma, dma((2, NZ)),
+        dma((2,)), dma((2, 2, 4)),
+        dma((2,)), dma((2, 2, 4)),
         dma, dma,
         dma, dma((NZ,)),
         dma, dma((NZ,)),
@@ -528,16 +564,18 @@
             sh((512, hidden), BF16),
             sh((hidden, 512), BF16),
         ),
-        in_specs=[any_spec, any_spec, pl.BlockSpec(memory_space=pltpu.VMEM)],
-        out_specs=(pl.BlockSpec(memory_space=pltpu.VMEM), any_spec, any_spec, any_spec),
+        in_specs=[any_spec] * 3,
+        out_specs=(any_spec,) * 4,
         scratch_shapes=[
             pltpu.VMEM((3, 512, hidden), BF16),
             pltpu.VMEM((2, 512, 512), BF16),
             pltpu.VMEM((512, hidden), BF16),
             pltpu.VMEM((512, hidden), BF16),
             pltpu.VMEM((hidden, 512), BF16),
-            dma((5,)),
-            dma((5,)),
+            pltpu.VMEM((NB, 512), F32),
+            pltpu.VMEM((NB, 512), BF16),
+            dma((7,)),
+            dma((6,)),
         ],
         compiler_params=pltpu.CompilerParams(vmem_limit_bytes=60 << 20),
         name="weight_grads",

time: 119 us -> 113 us (0.950); the launches traced: 118 us -> 113 us
  Pallas kernels: 117 us -> 112 us
    pallas_call x1, Pallas kernels: 109 us -> 106 us  [per_device(): pl.pallas_call(functools.partial(kernel, na, nb), out_shape=(sh((3, 512,...]
    pallas_call x1, Pallas kernels: 7.71 us -> 6.03 us  [per_device(): pl.pallas_call(weight_grads, out_shape=(sh((NB, 512), BF16), sh((512, hid...]
where the time goes in v3:
time: 113 us
  Pallas kernels  112 us (99%)
    pallas_call x1, Pallas kernels, per_device(): pl.pallas_call(functools.partial(kernel, na, nb), out_shape=(sh((3, 512,...  106 us
    pallas_call x1, Pallas kernels, per_device(): pl.pallas_call(weight_grads, out_shape=(sh((NB, 512), BF16), sh((512, hid...  6.03 us

profile of v3, /device:TPU:17, one launch (start us, length us, event | category | flops | bytes accessed | tf_op | source)
XLA Modules:
  0.0 113.3 jit_solution(3257573699994297557)
XLA Ops:
  0.6 106.4 %exchange.1 = (bf16[3,512,1792]{2,1,0:T(8,128)(2,1)}, bf16[2,8,2,32,512]{4,3,2,1,0:T(8,128)(2,1)}, f32[32,512]{1,0:T(8,128)}) custom-call(bf16[32,512]{1,0:T(8,128)(2,1)} %tok_in.1, bf16[32,512]{1,0:T(8,128)(2,1)} %og_in.1, bf16[512,1792]{1,0:T(8,128)(2,1)} %gw_in.1, bf16[512,1792]{1,0:T(8,128)(2,1)} %uw_in.1, bf16[1792,512]{1,0:T(8,128)(2,1)} %dw_in.1, ...), custom_call_target="tpu_custom_call" | custom-call | tf_op jit(solution)/shard_map/exchange/pallas_call | solution.py:548
  107.1 6.0 %weight_grads.1 = (bf16[32,512]{1,0:T(8,128)(2,1)}, bf16[512,1792]{1,0:T(8,128)(2,1)}, bf16[512,1792]{1,0:T(8,128)(2,1)}, bf16[1792,512]{1,0:T(8,128)(2,1)}) custom-call(bf16[3,512,1792]{2,1,0:T(8,128)(2,1)} %get-tuple-element.7.d_in, bf16[2,512,512]{2,1,0:T(8,128)(2,1)} %bitcast.2, f32[32,512]{1,0:T(8,128)} %get-tuple-element.9.ig_in), custom_call_target="tpu_custom_call" | custom-call | tf_op jit(solution)/shard_map/weight_grads/pallas_call | solution.py:559

commit v4 on v3

--- a/solution.py
+++ b/solution.py
@@ -38,7 +38,7 @@
     d_out, panel_out, ig_out,
     gw, uw, dw, panel,
     pa, pb, xa_s, xa_r, sa, ra, sb, rb, xb_s, xb_r,
-    ga, gb, ig_acc, sib_s, sib_r, ig_s, ig_r,
+    ga, gb, ig_acc, sib_s, sib_r, ig_s,
     lsem, dsem, tok_ss, tok_rs, fwd_ss, fwd_rs, xa_ss, xa_rs, za_ss, za_rs, zb_ss, zb_rs, xb_ss, xb_rs,
     gxa_ss, gxa_rs, gza_ss, gza_rs, gzb_ss, gzb_rs, gxb_ss, gxb_rs, sib_ss, sib_rs, ig_ss, ig_rs,
 ):
@@ -82,11 +82,11 @@
 
     def fwd_copy(p, j):
         blk = panel.at[p, chip(-j), core]
-        return remote(blk, blk, fwd_ss, fwd_rs.at[p, j], sib_dev)
+        return remote(blk, blk, fwd_ss, fwd_rs.at[p], sib_dev)
 
     def fwd_got(p, j):
         blk = panel.at[p, chip(-j), 1 - core]
-        return remote(blk, blk, fwd_ss, fwd_rs.at[p, j], sib_dev)
+        return remote(blk, blk, fwd_ss, fwd_rs.at[p], sib_dev)
 
     def send(p):
         loads[p].wait()
@@ -97,16 +97,15 @@
 
         fwd_copy(p, 0).start()
 
-    def forward(p):
-        @pl.loop(1, 8)
+    def forward(p, lo=1, hi=8):
+        @pl.loop(lo, hi)
         def _(j):
             tok_copy(p, j).wait_recv()
             fwd_copy(p, j).start()
 
     def gathered(p):
-        @pl.loop(0, 8)
-        def _(j):
-            fwd_got(p, j).wait_recv()
+        half = panel.at[p, pl.ds(0, 4)]
+        remote(half, half, fwd_ss, fwd_rs.at[p], sib_dev).wait_recv()
 
     def partial(m, rows, col):
         if m == 2:
@@ -134,6 +133,97 @@
         d = zp(k)
         ms = (pl.ds(0, 2), pl.ds(2, 1))[g]
         return remote(xa_s.at[d, ms], xa_r.at[d, ms], xa_ss, xa_rs.at[g, d], x_dev)
+
+    def hop(dst, own, recv, lo, hi, m0=0, m1=3):
+        width = own.shape[-1] // 2
+
+        @pl.loop(m0, m1)
+        def _(m):
+            for i in range(lo, hi):
+                c = pl.ds(i * width, width)
+                v = own[m, :, c]
+                for r in recv:
+                    v = v + dec(r[m, :, c])
+                dst[m, :, c] = enc(v) if dst.dtype == BF16 else v
+
+    class Ring:
+        def __init__(self, own, s, r, ss, rs):
+            self.own, self.s, self.r, self.ss, self.rs = own, s, r, ss, rs
+            self.half = s.shape[-1] // 2
+
+        def copy(self, step, d):
+            return self.copies(step, d, 0, 3, step - 1)
+
+        def copies(self, step, d, m0, m1, sem):
+            ms = pl.ds(m0, m1 - m0)
+            src, dst = self.s.at[d, step - 1, ms], self.r.at[d, step - 1, ms]
+            if step == 1:
+                c = pl.ds(d * self.half, self.half)
+                src, dst = src.at[:, :, c], dst.at[:, :, c]
+            return remote(src, dst, self.ss.at[min(step - 1, 1)], self.rs.at[d, sem], z_dev[d])
+
+        def first(self, m0, m1, sem):
+            for d in range(2):
+                own = self.own(zp(4 * (-1, 1)[d]))
+                hop(self.s.at[d, 0], own, (), d, d + 1, m0, m1)
+                self.copies(1, d, m0, m1, sem).start()
+
+        def second(self, m0, m1, sem):
+            for d in range(2):
+                own, src, got = self.own(zp(3 * (-1, 1)[d])), self.s.at[d, 1], self.r.at[d, 0]
+                self.copies(1, d, m0, m1, sem).wait_recv()
+                hop(src, own, (got,), d, d + 1, m0, m1)
+                hop(src, own, (), 1 - d, 2 - d, m0, m1)
+                self.copies(2, d, m0, m1, sem + 1).start()
+
+        def step(self, step, split=False):
+            for d in range(2):
+                own = self.own(zp((5 - step) * (-1, 1)[d]))
+                src = self.s.at[d, step - 1]
+                if step == 1:
+                    hop(src, own, (), d, d + 1)
+                else:
+                    if split:
+                        self.copies(step - 1, d, 0, 2, step - 2).wait_recv()
+                        self.copies(step - 1, d, 2, 3, step + 2).wait_recv()
+                    else:
+                        self.copy(step - 1, d).wait_recv()
+                    got = self.r.at[d, step - 2]
+                    if step == 2:
+                        hop(src, own, (got,), d, d + 1)
+                        hop(src, own, (), 1 - d, 2 - d)
+                    else:
+                        hop(src, own, (got,), 0, 2)
+                self.copy(step, d).start()
+
+        def finish(self, dst):
+            for d in range(2):
+                self.copy(4, d).wait_recv()
+            hop(dst, self.own(z), (self.r.at[0, 3], self.r.at[1, 3]), 0, 2)
+
+        def drain(self):
+            one, rest = self.s.at[0, 0], self.s.at[:, pl.ds(1, 3)]
+            remote(one, one, self.ss.at[0], self.rs.at[0, 0], z_dev[0]).wait_send()
+            remote(rest, rest, self.ss.at[1], self.rs.at[0, 0], z_dev[0]).wait_send()
+
+    ha = wa // 2
+    cols_a = (pl.ds(0, ha), pl.ds(ha, ha))
+    xs = (xo, xh)
+    rings_a = [
+        Ring(lambda d, c=cols_a[i]: pa.at[d, :, :, c], sa.at[i], ra.at[i], za_ss.at[i], za_rs.at[i]) for i in range(2)
+    ]
+    rings_b = [
+        Ring(lambda d, x=xs[i]: pb.at[d, pl.ds(3 * x, 3)], sb.at[i], rb.at[i], zb_ss.at[i], zb_rs.at[i])
+        for i in range(2)
+    ]
+
+    def step_a(step):
+        for ring in rings_a:
+            ring.step(step)
+
+    def step_b(step):
+        for ring in rings_b:
+            ring.step(step, split=step == 3)
 
     order = (4, 3, -3, 2, -2, 1, -1, 0)
     send(0)
@@ -145,88 +235,24 @@
     part_a((0, 1), xa_s, xo, enc)
     for k in order[:2]:
         xa_copy(k, 0).start()
+    forward(1, 1, 5)
     part_b((0, 1))
-    forward(1)
+    for ring in rings_b:
+        ring.first(0, 2, 0)
+    forward(1, 5)
     gathered(1)
     loads[4].wait()
     part_b((2,))
-
-    def hop(dst, own, recv, lo, hi):
-        width = own.shape[-1] // 2
-
-        @pl.loop(0, own.shape[0])
-        def _(m):
-            for i in range(lo, hi):
-                c = pl.ds(i * width, width)
-                v = own[m, :, c]
-                for r in recv:
-                    v = v + dec(r[m, :, c])
-                dst[m, :, c] = enc(v) if dst.dtype == BF16 else v
-
-    class Ring:
-        def __init__(self, own, s, r, ss, rs):
-            self.own, self.s, self.r, self.ss, self.rs = own, s, r, ss, rs
-            self.half = s.shape[-1] // 2
-
-        def copy(self, step, d):
-            src, dst = self.s.at[d, step - 1], self.r.at[d, step - 1]
-            if step == 1:
-                c = pl.ds(d * self.half, self.half)
-                src, dst = src.at[:, :, c], dst.at[:, :, c]
-            return remote(src, dst, self.ss.at[min(step - 1, 1)], self.rs.at[d, step - 1], z_dev[d])
-
-        def step(self, step):
-            for d in range(2):
-                own = self.own(zp((5 - step) * (-1, 1)[d]))
-                src = self.s.at[d, step - 1]
-                if step == 1:
-                    hop(src, own, (), d, d + 1)
-                else:
-                    self.copy(step - 1, d).wait_recv()
-                    got = self.r.at[d, step - 2]
-                    if step == 2:
-                        hop(src, own, (got,), d, d + 1)
-                        hop(src, own, (), 1 - d, 2 - d)
-                    else:
-                        hop(src, own, (got,), 0, 2)
-                self.copy(step, d).start()
-
-        def finish(self, dst):
-            for d in range(2):
-                self.copy(4, d).wait_recv()
-            hop(dst, self.own(z), (self.r.at[0, 3], self.r.at[1, 3]), 0, 2)
-
-        def drain(self):
-            one, rest = self.s.at[0, 0], self.s.at[:, pl.ds(1, 3)]
-            remote(one, one, self.ss.at[0], self.rs.at[0, 0], z_dev[0]).wait_send()
-            remote(rest, rest, self.ss.at[1], self.rs.at[0, 0], z_dev[0]).wait_send()
-
-    ha = wa // 2
-    cols_a = (pl.ds(0, ha), pl.ds(ha, ha))
-    xs = (xo, xh)
-    rings_a = [
-        Ring(lambda d, c=cols_a[i]: pa.at[d, :, :, c], sa.at[i], ra.at[i], za_ss.at[i], za_rs.at[i]) for i in range(2)
-    ]
-    rings_b = [
-        Ring(lambda d, x=xs[i]: pb.at[d, pl.ds(3 * x, 3)], sb.at[i], rb.at[i], zb_ss.at[i], zb_rs.at[i])
-        for i in range(2)
-    ]
-
-    def step_a(step):
-        for ring in rings_a:
-            ring.step(step)
-
-    def step_b(step):
-        for ring in rings_b:
-            ring.step(step)
-
-    step_b(1)
+    for ring in rings_b:
+        ring.first(2, 3, 4)
     part_a((2,), xa_s, xo, enc)
     for k in order[:2]:
         xa_copy(k, 1).start()
     for k in order[2:]:
         for g in range(2):
             xa_copy(k, g).start()
+    for ring in rings_b:
+        ring.second(0, 2, 0)
     part_a((0, 1, 2), pa, xh, lambda v: v)
 
     def take_x(k):
@@ -235,7 +261,8 @@
         d = zp(k)
         hop(pa.at[d], pa.at[d], (xa_r.at[d],), 0, 2)
 
-    step_b(2)
+    for ring in rings_b:
+        ring.second(2, 3, 4)
     take_x(4)
     step_a(1)
     for s, ks in ((2, (3, -3)), (3, (2, -2))):
@@ -267,19 +294,6 @@
             dst[1, :, tile(i)] = (hid_grad * up * sig * (1.0 + gate * (1.0 - sig))).astype(BF16)
             dst[2, :, tile(i)] = (hid_grad * act).astype(BF16)
 
-    xb_copy.wait()
-    hop(own_b, own_b, (xb_r,), 0, 2)
-    local(own_b, gb.at[z, pl.ds(3 * xh, 3)], nb, na)
-
-    def gxb_copy(x):
-        blk = gb.at[z, pl.ds(3 * x, 3)]
-        return remote(blk, blk, gxb_ss, gxb_rs, x_dev)
-
-    gxb_copy(xh).start()
-    for i in range(2):
-        rings_a[i].finish(pa.at[z, :, :, cols_a[i]])
-    local(pa.at[z], ga.at[z, xh], na, 0)
-
     def halves(blk, step, d, width):
         return blk.at[:, :, pl.ds(d * (width // 2), width // 2)] if step == 4 else blk
 
@@ -296,6 +310,21 @@
         blk = gb.at[zp((step if got else step - 1) * (1, -1)[d]), pl.ds(3 * xs[i], 3)]
         blk = halves(blk, step, d, wb)
         return remote(blk, blk, gzb_ss.at[step // 4], gzb_rs.at[i, d, step - 1], z_dev[d])
+
+    xb_copy.wait()
+    hop(own_b, own_b, (xb_r,), 0, 2)
+    local(own_b, gb.at[z, pl.ds(3 * xh, 3)], nb, na)
+
+    def gxb_copy(x):
+        blk = gb.at[z, pl.ds(3 * x, 3)]
+        return remote(blk, blk, gxb_ss, gxb_rs, x_dev)
+
+    gxb_copy(xh).start()
+    for d in range(2):
+        gzb_copy(1, 1, d).start()
+    for i in range(2):
+        rings_a[i].finish(pa.at[z, :, :, cols_a[i]])
+    local(pa.at[z], ga.at[z, xh], na, 0)
 
     def keep_a(k, x):
         d = zp(k)
@@ -316,8 +345,6 @@
     for i in range(2):
         for d in range(2):
             gza_copy(i, 1, d).start()
-    for d in range(2):
-        gzb_copy(1, 1, d).start()
     for i in range(2):
         gxa_copy(i, 0).start()
     keep_a(0, xh).start()
@@ -348,16 +375,14 @@
         for k in ks:
             d = zp(k)
             sib_copy(d).wait_recv()
-            v = ig_acc[d, core] + sib_r[d].astype(F32)
-            ig_acc[d, core] = v
-            ig_s[d] = v.astype(BF16)
+            ig_s[d] = (ig_acc[d, core] + sib_r[d].astype(F32)).astype(BF16)
 
             @pl.when(d != q)
             def _():
                 ig_copy((d - q + 8) % 8).start()
 
     def ig_copy(j):
-        return remote(ig_s.at[chip(j)], ig_r.at[j], ig_ss, ig_rs.at[j], peer(j))
+        return remote(ig_s.at[chip(j)], ig_out.at[j], ig_ss, ig_rs, peer(j))
 
     def sib_copy(d):
         return remote(sib_s.at[d], sib_r.at[d], sib_ss, sib_rs.at[d], sib_dev)
@@ -427,6 +452,8 @@
     keep_bs(4)
     ig_rows((4,), a=False)
     ig_send((4,))
+    last = pltpu.make_async_copy(ig_s.at[q], ig_out.at[0], lsem.at[1])
+    last.start()
 
     sent(xa_s, gxa_ss)
     sent(sib_s, sib_ss)
@@ -436,15 +463,8 @@
     sent(sb.at[:, :, pl.ds(0, 3)], gzb_ss.at[0])
     gxb_copy(xh).wait_send()
 
-    @pl.loop(1, 8)
-    def _(j):
-        ig_copy(j).wait_recv()
-        ig_acc[q, core] += ig_r[j].astype(F32)
-
-    sent(ig_s.at[pl.ds(0, 7)], ig_ss)
-    last = pltpu.make_async_copy(ig_acc.at[q, core], ig_out, lsem.at[1])
-    last.start()
-
+    pieces = pl.ds(0, 7)
+    remote(ig_s.at[pieces], ig_out.at[pl.ds(1, 7)], ig_ss, ig_rs, x_dev).wait()
     pltpu.make_async_copy(ga, ga, dsem.at[0]).wait()
     pltpu.make_async_copy(gb, gb, dsem.at[1]).wait()
     keep_panel.wait()
@@ -486,7 +506,7 @@
             dst[:, c] = dot(panel[0], d[m, :, c], 0, 0).astype(BF16)
         store(dst, out)
     loads[6].wait()
-    ig_b[...] = ig_v[...].astype(BF16)
+    ig_b[...] = sum(ig_v[j].astype(F32) for j in range(8)).astype(BF16)
     store(ig_b, ig_out)
     loads[4].wait()
     loads[5].wait()
@@ -529,25 +549,24 @@
         pltpu.VMEM((NZ, NB, 512), BF16),
         pltpu.VMEM((NZ, NB, 512), BF16),
         pltpu.VMEM((NZ, NB, 512), BF16),
-        pltpu.VMEM((NZ, NB, 512), BF16),
         dma((5,)), dma((2,)),
         dma, dma((2, 8)),
-        dma, dma((2, 8)),
+        dma, dma((2,)),
         dma, dma((2, NZ)),
         dma((2, 2)), dma((2, 2, 4)),
-        dma((2, 2)), dma((2, 2, 4)),
+        dma((2, 2)), dma((2, 2, 6)),
         dma, dma,
         dma, dma((2, NZ)),
         dma((2,)), dma((2, 2, 4)),
         dma((2,)), dma((2, 2, 4)),
         dma, dma,
         dma, dma((NZ,)),
-        dma, dma((NZ,)),
+        dma, dma,
     ]
     any_spec = pl.BlockSpec(memory_space=pl.ANY)
     deltas, panel, ig_sum = pl.pallas_call(
         functools.partial(kernel, na, nb),
-        out_shape=(sh((3, 512, hidden), BF16), sh((2, NZ, 2, NB, 512), BF16), sh((NB, 512), F32)),
+        out_shape=(sh((3, 512, hidden), BF16), sh((2, NZ, 2, NB, 512), BF16), sh((8, NB, 512), BF16)),
         in_specs=[any_spec] * 5 + [pl.BlockSpec(memory_space=pltpu.VMEM)],
         out_specs=[any_spec] * 3,
         scratch_shapes=scratch,
@@ -572,7 +591,7 @@
             pltpu.VMEM((512, hidden), BF16),
             pltpu.VMEM((512, hidden), BF16),
             pltpu.VMEM((hidden, 512), BF16),
-            pltpu.VMEM((NB, 512), F32),
+            pltpu.VMEM((8, NB, 512), BF16),
             pltpu.VMEM((NB, 512), BF16),
             dma((7,)),
             dma((6,)),

time: 113 us -> 110 us (0.973)
  Pallas kernels: 112 us -> 109 us
    pallas_call x1, Pallas kernels: 106 us -> 103 us  [per_device(): pl.pallas_call(functools.partial(kernel, na, nb), out_shape=(sh((3, 512,...]
where the time goes in v4:
time: 110 us
  Pallas kernels  109 us (99%)
    pallas_call x1, Pallas kernels, per_device(): pl.pallas_call(functools.partial(kernel, na, nb), out_shape=(sh((3, 512,...  103 us
    pallas_call x1, Pallas kernels, per_device(): pl.pallas_call(weight_grads, out_shape=(sh((NB, 512), BF16), sh((512, hid...  6.07 us

profile of v4, /device:TPU:17, one launch (start us, length us, event | category | flops | bytes accessed | tf_op | source)
XLA Modules:
  0.0 110.1 jit_solution(7387943098171581573)
XLA Ops:
  0.6 103.3 %exchange.1 = (bf16[3,512,1792]{2,1,0:T(8,128)(2,1)}, bf16[2,8,2,32,512]{4,3,2,1,0:T(8,128)(2,1)}, bf16[8,32,512]{2,1,0:T(8,128)(2,1)}) custom-call(bf16[32,512]{1,0:T(8,128)(2,1)} %tok_in.1, bf16[32,512]{1,0:T(8,128)(2,1)} %og_in.1, bf16[512,1792]{1,0:T(8,128)(2,1)} %gw_in.1, bf16[512,1792]{1,0:T(8,128)(2,1)} %uw_in.1, bf16[1792,512]{1,0:T(8,128)(2,1)} %dw_in.1, ...), custom_call_target="tpu_custom_call" | custom-call | tf_op jit(solution)/shard_map/exchange/pallas_call | solution.py:567
  103.9 6.1 %weight_grads.1 = (bf16[32,512]{1,0:T(8,128)(2,1)}, bf16[512,1792]{1,0:T(8,128)(2,1)}, bf16[512,1792]{1,0:T(8,128)(2,1)}, bf16[1792,512]{1,0:T(8,128)(2,1)}) custom-call(bf16[3,512,1792]{2,1,0:T(8,128)(2,1)} %get-tuple-element.7.d_in, bf16[2,512,512]{2,1,0:T(8,128)(2,1)} %bitcast.2, bf16[8,32,512]{2,1,0:T(8,128)(2,1)} %get-tuple-element.9.ig_in), custom_call_target="tpu_custom_call" | custom-call | tf_op jit(solution)/shard_map/weight_grads/pallas_call | solution.py:578

commit v5 on v4

--- a/solution.py
+++ b/solution.py
@@ -34,9 +34,9 @@
 
 def kernel(
     na, nb,
-    tok_in, og_in, gw_in, uw_in, dw_in, cap_in,
+    tok_in, og_in, gw_in, uw_in, dw_in, cap_hbm,
     d_out, panel_out, ig_out,
-    gw, uw, dw, panel,
+    gw, uw, dw, panel, cap_in,
     pa, pb, xa_s, xa_r, sa, ra, sb, rb, xb_s, xb_r,
     ga, gb, ig_acc, sib_s, sib_r, ig_s,
     lsem, dsem, tok_ss, tok_rs, fwd_ss, fwd_rs, xa_ss, xa_rs, za_ss, za_rs, zb_ss, zb_rs, xb_ss, xb_rs,
@@ -65,6 +65,7 @@
         pltpu.make_async_copy(gw_in, gw, lsem.at[2]),
         pltpu.make_async_copy(uw_in, uw, lsem.at[3]),
         pltpu.make_async_copy(dw_in, dw, lsem.at[4]),
+        pltpu.make_async_copy(cap_hbm, cap_in, lsem.at[5]),
     ]
     for c in loads:
         c.start()
@@ -132,7 +133,7 @@
     def xa_copy(k, g):
         d = zp(k)
         ms = (pl.ds(0, 2), pl.ds(2, 1))[g]
-        return remote(xa_s.at[d, ms], xa_r.at[d, ms], xa_ss, xa_rs.at[g, d], x_dev)
+        return remote(xa_s.at[d, ms], xa_r.at[d, ms], xa_ss, xa_rs.at[d], x_dev)
 
     def hop(dst, own, recv, lo, hi, m0=0, m1=3):
         width = own.shape[-1] // 2
@@ -242,6 +243,7 @@
     forward(1, 5)
     gathered(1)
     loads[4].wait()
+    loads[5].wait()
     part_b((2,))
     for ring in rings_b:
         ring.first(2, 3, 4)
@@ -256,9 +258,8 @@
     part_a((0, 1, 2), pa, xh, lambda v: v)
 
     def take_x(k):
-        for g in range(2):
-            xa_copy(k, g).wait_recv()
         d = zp(k)
+        remote(xa_s.at[d], xa_r.at[d], xa_ss, xa_rs.at[d], x_dev).wait_recv()
         hop(pa.at[d], pa.at[d], (xa_r.at[d],), 0, 2)
 
     for ring in rings_b:
@@ -302,9 +303,12 @@
         blk = halves(blk, step, d, ha)
         return remote(blk, blk, gza_ss.at[step // 4], gza_rs.at[i, d, step - 1], z_dev[d])
 
-    def gxa_copy(i, k, got=False):
-        blk = ga.at[zp(k), xo if got else xh, :, :, cols_a[i]]
-        return remote(blk, blk, gxa_ss, gxa_rs.at[i, zp(k)], x_dev)
+    def phase(k):
+        return 0 if abs(k) < 3 else 1 if abs(k) == 3 else 2
+
+    def gxa_copy(i, k):
+        blk = ga.at[zp(k), xh, :, :, cols_a[i]]
+        return remote(blk, blk, gxa_ss, gxa_rs.at[phase(k)], x_dev)
 
     def gzb_copy(i, step, d, got=False):
         blk = gb.at[zp((step if got else step - 1) * (1, -1)[d]), pl.ds(3 * xs[i], 3)]
@@ -323,8 +327,12 @@
     for d in range(2):
         gzb_copy(1, 1, d).start()
     for i in range(2):
-        rings_a[i].finish(pa.at[z, :, :, cols_a[i]])
-    local(pa.at[z], ga.at[z, xh], na, 0)
+        own_a = pa.at[z, :, :, cols_a[i]]
+        rings_a[i].finish(own_a)
+        local(own_a, ga.at[z, xh, :, :, cols_a[i]], na // 2, i * (na // 2))
+        for d in range(2):
+            gza_copy(i, 1, d).start()
+        gxa_copy(i, 0).start()
 
     def keep_a(k, x):
         d = zp(k)
@@ -342,11 +350,6 @@
         for x in range(2):
             keep_b(k, x).start()
 
-    for i in range(2):
-        for d in range(2):
-            gza_copy(i, 1, d).start()
-    for i in range(2):
-        gxa_copy(i, 0).start()
     keep_a(0, xh).start()
     keep_panel = pltpu.make_async_copy(panel, panel_out, lsem.at[0])
     keep_panel.start()
@@ -363,18 +366,19 @@
                 v = v + dot(rows(lambda d, x: gb[d, 3 * x + m]), wt[:, wa:], 1, 1)
         for n_k, k in enumerate(ks):
             part = v[n_k * 2 * NB : (n_k + 1) * 2 * NB].reshape(2, NB, 512)
-            ig_acc[zp(k)] = part if a else ig_acc[zp(k)] + part
-        if not b:
+            ig_acc[zp(k)] = part if b else ig_acc[zp(k)] + part
+        if not a:
             return
         for k in ks:
             d = zp(k)
             sib_s[d] = ig_acc[d, 1 - core].astype(BF16)
-            sib_copy(d).start()
-
-    def ig_send(ks):
+            sib_copy(k).start()
+
+    def ig_send(ks, n):
+        blocks = sib_s.at[pl.ds(0, len(ks))]
+        remote(blocks, blocks, sib_ss, sib_rs.at[n], sib_dev).wait_recv()
         for k in ks:
             d = zp(k)
-            sib_copy(d).wait_recv()
             ig_s[d] = (ig_acc[d, core] + sib_r[d].astype(F32)).astype(BF16)
 
             @pl.when(d != q)
@@ -384,13 +388,15 @@
     def ig_copy(j):
         return remote(ig_s.at[chip(j)], ig_out.at[j], ig_ss, ig_rs, peer(j))
 
-    def sib_copy(d):
-        return remote(sib_s.at[d], sib_r.at[d], sib_ss, sib_rs.at[d], sib_dev)
-
-    def take_gx(k):
-        for i in range(2):
-            gxa_copy(i, k, True).wait_recv()
-        keep_a(k, xo).start()
+    def sib_copy(k):
+        d = zp(k)
+        return remote(sib_s.at[d], sib_r.at[d], sib_ss, sib_rs.at[phase(k)], sib_dev)
+
+    def take_gx(ks, n):
+        blocks = xa_s.at[pl.ds(0, len(ks))]
+        remote(blocks, blocks, gxa_ss, gxa_rs.at[n], x_dev).wait_recv()
+        for k in ks:
+            keep_a(k, xo).start()
 
     def forward_a(step):
         for i in range(2):
@@ -429,8 +435,7 @@
     for ring in rings_a + rings_b:
         ring.drain()
     early = (0, 1, -1, 2, -2)
-    for k in early:
-        take_gx(k)
+    take_gx(early, 0)
     ig_rows(early)
     for i in range(2):
         for d in range(2):
@@ -439,19 +444,18 @@
     keep_a(4, xh).start()
     forward_b(1, 4)
     forward_b(0, 4)
-    ig_send(early)
-    for k in (3, -3):
-        take_gx(k)
+    ig_send(early, 0)
+    take_gx((3, -3), 1)
     ig_rows((3, -3))
-    ig_send((3, -3))
-    take_gx(4)
-    ig_rows((4,), b=False)
+    ig_send((3, -3), 1)
     for i in (1, 0):
         for d in range(2):
             gzb_copy(i, 4, d, True).wait_recv()
     keep_bs(4)
     ig_rows((4,), a=False)
-    ig_send((4,))
+    take_gx((4,), 2)
+    ig_rows((4,), b=False)
+    ig_send((4,), 2)
     last = pltpu.make_async_copy(ig_s.at[q], ig_out.at[0], lsem.at[1])
     last.start()
 
@@ -533,6 +537,7 @@
         pltpu.VMEM((512, hidden), BF16),
         pltpu.VMEM((hidden, 512), BF16),
         pltpu.VMEM((2, NZ, 2, NB, 512), BF16),
+        pltpu.VMEM((hidden // 128, 128), jnp.int32),
         pltpu.VMEM((NZ, 3, NB, wa), F32),
         pltpu.VMEM((NZ, 6, NB, wb), F32),
         pltpu.VMEM((NZ, 3, NB, wa), BF16),
@@ -549,25 +554,25 @@
         pltpu.VMEM((NZ, NB, 512), BF16),
         pltpu.VMEM((NZ, NB, 512), BF16),
         pltpu.VMEM((NZ, NB, 512), BF16),
-        dma((5,)), dma((2,)),
+        dma((6,)), dma((2,)),
         dma, dma((2, 8)),
         dma, dma((2,)),
-        dma, dma((2, NZ)),
+        dma, dma((NZ,)),
         dma((2, 2)), dma((2, 2, 4)),
         dma((2, 2)), dma((2, 2, 6)),
         dma, dma,
-        dma, dma((2, NZ)),
+        dma, dma((3,)),
         dma((2,)), dma((2, 2, 4)),
         dma((2,)), dma((2, 2, 4)),
         dma, dma,
-        dma, dma((NZ,)),
+        dma, dma((3,)),
         dma, dma,
     ]
     any_spec = pl.BlockSpec(memory_space=pl.ANY)
     deltas, panel, ig_sum = pl.pallas_call(
         functools.partial(kernel, na, nb),
         out_shape=(sh((3, 512, hidden), BF16), sh((2, NZ, 2, NB, 512), BF16), sh((8, NB, 512), BF16)),
-        in_specs=[any_spec] * 5 + [pl.BlockSpec(memory_space=pltpu.VMEM)],
+        in_specs=[any_spec] * 6,
         out_specs=[any_spec] * 3,
         scratch_shapes=scratch,
         compiler_params=pltpu.CompilerParams(

time: 110 us -> 110 us (level)
  no operation moved by 1% of the time
where the time goes in v5:
time: 110 us
  Pallas kernels  109 us (99%)
    pallas_call x1, Pallas kernels, per_device(): pl.pallas_call(functools.partial(kernel, na, nb), out_shape=(sh((3, 512,...  103 us
    pallas_call x1, Pallas kernels, per_device(): pl.pallas_call(weight_grads, out_shape=(sh((NB, 512), BF16), sh((512, hid...  6.07 us

profile of v5, /device:TPU:17, one launch (start us, length us, event | category | flops | bytes accessed | tf_op | source)
XLA Modules:
  0.0 109.6 jit_solution(10993741135090429947)
XLA Ops:
  0.6 102.7 %exchange.1 = (bf16[3,512,1792]{2,1,0:T(8,128)(2,1)}, bf16[2,8,2,32,512]{4,3,2,1,0:T(8,128)(2,1)}, bf16[8,32,512]{2,1,0:T(8,128)(2,1)}) custom-call(bf16[32,512]{1,0:T(8,128)(2,1)} %tok_in.1, bf16[32,512]{1,0:T(8,128)(2,1)} %og_in.1, bf16[512,1792]{1,0:T(8,128)(2,1)} %gw_in.1, bf16[512,1792]{1,0:T(8,128)(2,1)} %uw_in.1, bf16[1792,512]{1,0:T(8,128)(2,1)} %dw_in.1, ...), custom_call_target="tpu_custom_call" | custom-call | tf_op jit(solution)/shard_map/exchange/pallas_call | solution.py:572
  103.3 6.1 %weight_grads.1 = (bf16[32,512]{1,0:T(8,128)(2,1)}, bf16[512,1792]{1,0:T(8,128)(2,1)}, bf16[512,1792]{1,0:T(8,128)(2,1)}, bf16[1792,512]{1,0:T(8,128)(2,1)}) custom-call(bf16[3,512,1792]{2,1,0:T(8,128)(2,1)} %get-tuple-element.7.d_in, bf16[2,512,512]{2,1,0:T(8,128)(2,1)} %bitcast.2, bf16[8,32,512]{2,1,0:T(8,128)(2,1)} %get-tuple-element.9.ig_in), custom_call_target="tpu_custom_call" | custom-call | tf_op jit(solution)/shard_map/weight_grads/pallas_call | solution.py:583

commit v6 on v5

--- a/solution.py
+++ b/solution.py
@@ -228,8 +228,9 @@
 
     order = (4, 3, -3, 2, -2, 1, -1, 0)
     send(0)
+    forward(0, 1, 2)
     send(1)
-    forward(0)
+    forward(0, 2)
     gathered(0)
     loads[2].wait()
     loads[3].wait()
@@ -422,8 +423,8 @@
     forward_b(1, 2)
     forward_a(3)
     forward_b(0, 2)
+    forward_b(1, 3)
     forward_a(4)
-    forward_b(1, 3)
     forward_b(0, 3)
 
     def sent(ref, sem):

time: 110 us -> 109 us (level)
  no operation moved by 1% of the time
where the time goes in v6:
time: 109 us
  Pallas kernels  108 us (99%)
    pallas_call x1, Pallas kernels, per_device(): pl.pallas_call(functools.partial(kernel, na, nb), out_shape=(sh((3, 512,...  102 us
    pallas_call x1, Pallas kernels, per_device(): pl.pallas_call(weight_grads, out_shape=(sh((NB, 512), BF16), sh((512, hid...  6.07 us

profile of v6, /device:TPU:17, one launch (start us, length us, event | category | flops | bytes accessed | tf_op | source)
XLA Modules:
  0.0 109.0 jit_solution(15334302973700619870)
XLA Ops:
  0.6 102.1 %exchange.1 = (bf16[3,512,1792]{2,1,0:T(8,128)(2,1)}, bf16[2,8,2,32,512]{4,3,2,1,0:T(8,128)(2,1)}, bf16[8,32,512]{2,1,0:T(8,128)(2,1)}) custom-call(bf16[32,512]{1,0:T(8,128)(2,1)} %tok_in.1, bf16[32,512]{1,0:T(8,128)(2,1)} %og_in.1, bf16[512,1792]{1,0:T(8,128)(2,1)} %gw_in.1, bf16[512,1792]{1,0:T(8,128)(2,1)} %uw_in.1, bf16[1792,512]{1,0:T(8,128)(2,1)} %dw_in.1, ...), custom_call_target="tpu_custom_call" | custom-call | tf_op jit(solution)/shard_map/exchange/pallas_call | solution.py:573
  102.8 6.1 %weight_grads.1 = (bf16[32,512]{1,0:T(8,128)(2,1)}, bf16[512,1792]{1,0:T(8,128)(2,1)}, bf16[512,1792]{1,0:T(8,128)(2,1)}, bf16[1792,512]{1,0:T(8,128)(2,1)}) custom-call(bf16[3,512,1792]{2,1,0:T(8,128)(2,1)} %get-tuple-element.7.d_in, bf16[2,512,512]{2,1,0:T(8,128)(2,1)} %bitcast.2, bf16[8,32,512]{2,1,0:T(8,128)(2,1)} %get-tuple-element.9.ig_in), custom_call_target="tpu_custom_call" | custom-call | tf_op jit(solution)/shard_map/weight_grads/pallas_call | solution.py:584

commit v7 on v6

--- a/solution.py
+++ b/solution.py
@@ -426,6 +426,7 @@
     forward_b(1, 3)
     forward_a(4)
     forward_b(0, 3)
+    forward_b(1, 4)
 
     def sent(ref, sem):
         remote(ref, ref, sem, gxb_rs, x_dev).wait_send()
@@ -443,7 +444,6 @@
             gza_copy(i, 4, d, True).wait_recv()
         gxa_copy(i, 4).start()
     keep_a(4, xh).start()
-    forward_b(1, 4)
     forward_b(0, 4)
     ig_send(early, 0)
     take_gx((3, -3), 1)

time: 109 us -> 109 us (level)
  no operation moved by 1% of the time
where the time goes in v7:
time: 109 us
  Pallas kernels  108 us (99%)
    pallas_call x1, Pallas kernels, per_device(): pl.pallas_call(functools.partial(kernel, na, nb), out_shape=(sh((3, 512,...  102 us
    pallas_call x1, Pallas kernels, per_device(): pl.pallas_call(weight_grads, out_shape=(sh((NB, 512), BF16), sh((512, hid...  6.07 us

profile of v7, /device:TPU:17, one launch (start us, length us, event | category | flops | bytes accessed | tf_op | source)
XLA Modules:
  0.0 109.0 jit_solution(9728772934462503149)
XLA Ops:
  0.6 102.1 %exchange.1 = (bf16[3,512,1792]{2,1,0:T(8,128)(2,1)}, bf16[2,8,2,32,512]{4,3,2,1,0:T(8,128)(2,1)}, bf16[8,32,512]{2,1,0:T(8,128)(2,1)}) custom-call(bf16[32,512]{1,0:T(8,128)(2,1)} %tok_in.1, bf16[32,512]{1,0:T(8,128)(2,1)} %og_in.1, bf16[512,1792]{1,0:T(8,128)(2,1)} %gw_in.1, bf16[512,1792]{1,0:T(8,128)(2,1)} %uw_in.1, bf16[1792,512]{1,0:T(8,128)(2,1)} %dw_in.1, ...), custom_call_target="tpu_custom_call" | custom-call | tf_op jit(solution)/shard_map/exchange/pallas_call | solution.py:573
  102.8 6.1 %weight_grads.1 = (bf16[32,512]{1,0:T(8,128)(2,1)}, bf16[512,1792]{1,0:T(8,128)(2,1)}, bf16[512,1792]{1,0:T(8,128)(2,1)}, bf16[1792,512]{1,0:T(8,128)(2,1)}) custom-call(bf16[3,512,1792]{2,1,0:T(8,128)(2,1)} %get-tuple-element.7.d_in, bf16[2,512,512]{2,1,0:T(8,128)(2,1)} %bitcast.2, bf16[8,32,512]{2,1,0:T(8,128)(2,1)} %get-tuple-element.9.ig_in), custom_call_target="tpu_custom_call" | custom-call | tf_op jit(solution)/shard_map/weight_grads/pallas_call | solution.py:584
